TPU v7x, 512 devices: a whole 4x4x16 slice. The times are simulated.
512 devices in a mesh: seq: 64 (over y, z), head: 8 (over x, core).
Axes of the slice: x: 4, y: 4, z: 16, core: 2. Of those that a mesh axis runs over, the one named last changes fastest.
Arguments:
- queries: bfloat16 [65536, 16, 128], P(('seq', 'head')), may hold values from -6 to 6
- keys: bfloat16 [65536, 16, 2, 128], P(('seq', 'head')), may hold values from -6 to 6
- values: bfloat16 [65536, 16, 2, 128], P(('seq', 'head')), may hold values from -6 to 6
- betas: bfloat16 [65536, 16, 2], P(('seq', 'head')), may hold values from 0 to 2
- gate: bfloat16 [65536, 16, 128], P(('seq', 'head')), may hold values from -6 to 6
- gain: float32 [16, 128], P('head'), may hold values from 0.1 to 1.9
Outputs:
- mixed: bfloat16 [65536, 16, 128], P(('seq', 'head'))
All inputs are finite; a program needn't handle non-finite values.
Results may differ from a plain program's by a relative error of at most 0.0012.
Values may be sent and summed in bfloat16 or wider, within the bound.
A program may use at most 128 MiB of HBM per device.

v0:
```python
import jax
import jax.numpy as jnp
from jax import lax
from jax.sharding import PartitionSpec as P

exact_prec = lax.Precision.HIGHEST


def entering(part, axis, combine, identity):
    place = lax.axis_index(axis)
    gathered = jax.tree.map(lambda a: lax.all_gather(a, axis), part)
    state = jax.tree.map(lambda a, e: jnp.zeros_like(a) + jnp.asarray(e, a.dtype), part, identity)

    def one(lap, state):
        return combine(
            state, jax.tree.map(lambda a: lax.dynamic_index_in_dim(a, lap, 0, False), gathered)
        )

    return lax.fori_loop(0, place, one, state)


def unit_rows(matrix):
    return matrix * lax.rsqrt(jnp.sum(matrix * matrix, axis=-1, keepdims=True) + 1e-06)


def compose_pair(earlier, later):
    early_tr, early_st = earlier
    late_tr, late_st = later
    joined_tr = jnp.einsum("hkl,hlm->hkm", late_tr, early_tr, precision=exact_prec)
    joined_st = jnp.einsum("hkl,hlm->hkm", late_tr, early_st, precision=exact_prec) + late_st
    return (joined_tr, joined_st)


def carry_in(transit_all, local_state, start_tr, start_st):
    _, incoming = entering((transit_all, local_state), "seq", compose_pair, (start_tr, start_st))
    return incoming


def local(queries, keys, values, betas, gate, gain):
    query_g, key_g, value_g, beta_g = (
        lax.all_to_all(queries, "head", split_axis=1, concat_axis=0, tiled=True),
        lax.all_to_all(keys, "head", split_axis=1, concat_axis=0, tiled=True),
        lax.all_to_all(values, "head", split_axis=1, concat_axis=0, tiled=True),
        lax.all_to_all(betas, "head", split_axis=1, concat_axis=0, tiled=True),
    )
    row_count, heads_here, steps_per, head_width = key_g.shape
    substeps = row_count * steps_per
    block_len = min(128, substeps)
    group_count = substeps // block_len
    tok_block = block_len // steps_per
    keys_f = unit_rows(jnp.transpose(key_g, (1, 0, 2, 3)).astype(jnp.float32)).reshape(
        heads_here, group_count, block_len, head_width
    )
    vals_f = (
        jnp.transpose(value_g, (1, 0, 2, 3))
        .astype(jnp.float32)
        .reshape(heads_here, group_count, block_len, head_width)
    )
    spike_intensity = (
        jnp.transpose(beta_g, (1, 0, 2))
        .astype(jnp.float32)
        .reshape(heads_here, group_count, block_len)
    )
    query_f = (
        jnp.transpose(query_g, (1, 0, 2))
        .astype(jnp.float32)
        .reshape(heads_here, group_count, tok_block, head_width)
    )
    sub_index = jnp.arange(block_len)
    tok_index = jnp.arange(tok_block)
    strict_lower = sub_index[:, None] > sub_index[None, :]
    visible = sub_index[None, :] <= steps_per * tok_index[:, None] + steps_per - 1
    grams = jnp.einsum("hcik,hcjk->hcij", keys_f, keys_f, precision=exact_prec)
    system = jnp.eye(block_len, dtype=jnp.float32) + jnp.where(
        strict_lower, spike_intensity[..., None] * grams, 0.0
    )
    right_sides = jnp.concatenate(
        [spike_intensity[..., None] * keys_f, spike_intensity[..., None] * vals_f], axis=-1
    )
    solved = lax.linalg.triangular_solve(
        system, right_sides, left_side=True, lower=True, unit_diagonal=True
    )
    w_part = solved[..., :head_width]
    u_part = solved[..., head_width:]
    scores = jnp.where(
        visible, jnp.einsum("hctk,hcjk->hctj", query_f, keys_f, precision=exact_prec), 0.0
    )
    square_eye = jnp.eye(head_width, dtype=jnp.float32)
    transits = square_eye - jnp.einsum("hcik,hcil->hckl", keys_f, w_part, precision=exact_prec)
    per_group = tuple(
        (
            jnp.moveaxis(member, 1, 0)
            for member in (transits, w_part, u_part, keys_f, query_f, scores)
        )
    )
    start_tr = jnp.broadcast_to(square_eye, (heads_here, head_width, head_width))
    start_st = jnp.zeros((heads_here, head_width, head_width), jnp.float32)

    def group_out(carry_state, pieces):
        transit, w_group, u_group, keys_group, query_group, score_group = pieces
        fresh_vals = u_group - jnp.einsum(
            "hik,hkl->hil", w_group, carry_state, precision=exact_prec
        )
        step_out = jnp.einsum("htk,hkl->htl", query_group, carry_state, precision=exact_prec)
        step_out = step_out + jnp.einsum(
            "htj,hjl->htl", score_group, fresh_vals, precision=exact_prec
        )
        carry_state = carry_state + jnp.einsum(
            "hik,hil->hkl", keys_group, fresh_vals, precision=exact_prec
        )
        return (carry_state, step_out)

    def compose_local(carry, pieces):
        transit_all, carry_state = carry
        transit, w_group, u_group, keys_group = pieces[:4]
        fresh_vals = u_group - jnp.einsum(
            "hik,hkl->hil", w_group, carry_state, precision=exact_prec
        )
        carry_state = carry_state + jnp.einsum(
            "hik,hil->hkl", keys_group, fresh_vals, precision=exact_prec
        )
        transit_all = jnp.einsum("hkl,hlm->hkm", transit, transit_all, precision=exact_prec)
        return ((transit_all, carry_state), None)

    (transit_all, local_state), _ = lax.scan(compose_local, (start_tr, start_st), per_group)
    incoming = carry_in(transit_all, local_state, start_tr, start_st)
    _, group_outs = lax.scan(group_out, incoming, per_group)
    outputs = jnp.moveaxis(group_outs, 0, 1)
    outputs = outputs.reshape(heads_here, row_count, head_width)
    normed = (
        outputs
        * lax.rsqrt(jnp.mean(outputs * outputs, axis=-1, keepdims=True) + 1e-06)
        * gain[:, None, :]
    )
    token_normed = lax.all_to_all(
        jnp.transpose(normed, (1, 0, 2)), "head", split_axis=0, concat_axis=1, tiled=True
    )
    return (token_normed * jax.nn.silu(gate.astype(jnp.float32))).astype(jnp.bfloat16)


def solution(mesh):
    return jax.shard_map(
        local,
        mesh=mesh,
        in_specs=(
            P(("seq", "head"), None, None),
            P(("seq", "head"), None, None, None),
            P(("seq", "head"), None, None, None),
            P(("seq", "head"), None, None),
            P(("seq", "head"), None, None),
            P("head", None),
        ),
        out_specs=P(("seq", "head"), None, None),
        check_vma=False,
    )
```

profile of v0, /device:TPU:25, one launch (start us, length us, event | category | flops | bytes accessed | tf_op | source)
XLA Modules:
  0.0 924.5 jit_solution(17557681545650283605)
XLA Ops:
  6.5 5.0 all-to-all-start.1
  11.5 3.3 copy.61
  16.1 4.2 all-to-all-start
  20.3 2.0 copy.65
  23.3 12.1 %all-to-all-done = bf16[128,16,2,128]{3,2,0,1:T(2,128)(2,1)S(1)} async-done(((bf16[128,16,2,128]{3,2,0,1:T(2,128)(2,1)}), bf16[128,16,2,128]{3,2,0,1:T(2,128)(2,1)S(1)}, u32[]{:S(2)}, u32[]{:S(2)}) %all-to-all-start) | async-done | bytes 1048608 | tf_op jit(solution)/shard_map/all_to_all | solution.py:42
  35.4 4.3 all-to-all-start.2
  40.8 2.3 multiply_reduce_fusion
  43.2 2.6 broadcast_multiply_fusion.2
  45.8 5.8 add_bitcast_fusion
  51.7 315.8 %custom-call.3 = f32[2,16,1,128,128]{3,4,2,1,0:T(8,128)} custom-call(f32[2,16,1,128,128]{4,3,2,1,0:T(8,128)} %add_bitcast_fusion), custom_call_target="InvertDiagBlocksLowerTriangular" | custom-call | tf_op jit(solution)/shard_map/triangular_solve | solution.py:80
  370.1 3.8 fusion.32
  373.9 4.8 subtract_bitcast_fusion
  379.3 1.5 copy.71
  380.8 1.5 copy.72
  382.2 1.8 copy.70
  384.1 58.5 %while.42 = (s32[]{:T(128)}, f32[2,128,128]{2,1,0:T(8,128)S(1)}, f32[2,128,128]{2,1,0:T(8,128)S(1)}, f32[16,2,128,128]{3,2,0,1:T(8,128)}, f32[16,2,128,128]{2,3,...) while((s32[]{:T(128)}, f32[2,128,128]{2,1,0:T(8,128)S(1)}, ...), condition=%wide.region_2.3_spmd.clone.clone, body=%wide.region_1.2_spmd.clone.sunk.clone | while | flops 151126016 | bytes 1706072 | solution.py:125
  445.0 4.8 all-to-all-start.3
  449.9 9.5 %all-to-all-done.3 = bf16[128,16,128]{2,0,1:T(8,128)(2,1)} async-done(((bf16[128,16,128]{2,0,1:T(8,128)(2,1)}), bf16[128,16,128]{2,0,1:T(8,128)(2,1)}, u32[]{:S(2)}, u32[]{:S(2)}) %all-to-all-start.3) | async-done | bytes 524320 | tf_op jit(solution)/shard_map/all_to_all | solution.py:41
  461.6 3.3 fusion.41
  464.9 129.9 %all-gather.5.cloned.1.call-done = f32[128,128,128]{2,1,0:T(8,128)} async-done(((f32[2,128,128]{2,1,0:T(8,128)}), f32[128,128,128]{2,1,0:T(8,128)}) %all-gather.5.cloned.1.call-update) | async-done | bytes 8388624 | tf_op jit(solution)/shard_map/all_gather | solution.py:11
  594.8 154.8 %all-gather.7.cloned.1.call-done = f32[128,128,128]{2,1,0:T(8,128)} async-done(((f32[2,128,128]{2,1,0:T(8,128)}), f32[128,128,128]{2,1,0:T(8,128)}) %all-gather.7.cloned.1.call-update) | async-done | bytes 8388624 | tf_op jit(solution)/shard_map/all_gather | solution.py:11
  749.6 62.0 %while.40 = (s32[]{:T(128)}, f32[2,128,128]{2,1,0:T(8,128)S(1)}, s32[]{:T(128)}, f32[64,2,128,128]{3,2,1,0:T(8,128)}, f32[64,2,128,128]{3,2,1,0:T(8,128)}) while((s32[]{:T(128)}, f32[2,128,128]{2,1,0:T(8,128)S(1)}, s32[]{:T(128)}, f32[64,2,128,128]{3,2,1,0:T(8,128)}, f32[64,2,128,128]{3,2,1,0:T(8,128)}) %tuple.89), condition=%wide.region_4.5_spmd.clone, body=%wide.region_3.4_spmd.sunk.clone | while | flops 50364420 | bytes 787551 | solution.py:19
  811.6 74.5 %while.41 = (s32[]{:T(128)}, f32[2,128,128]{2,1,0:T(8,128)S(1)}, f32[16,2,64,128]{3,2,0,1:T(8,128)S(1)}, f32[16,2,128,128]{2,3,1,0:T(8,128)}, f32[16,2,128,128]{...) while((s32[]{:T(128)}, f32[2,128,128]{2,1,0:T(8,128)S(1)}, ...), condition=%wide.region_6.7_spmd.clone, body=%wide.region_5.6_spmd.sunk.clone | while | flops 151076864 | bytes 1641557 | solution.py:127
  887.7 27.4 %all_to_all.63 = f32[1024,2,128]{2,1,0:T(2,128)S(1)} all-to-all(f32[1024,2,128]{2,1,0:T(2,128)S(1)} %copy.82), channel_id=1, replica_groups=mesh['seq'=64,'head'=8] {'head'}, dimensions={0} | all-to-all | bytes 2097152 | tf_op jit(solution)/shard_map/all_to_all | solution.py:135
  (276 shorter events, 206.6 us)
Async XLA Ops:
  6.5 9.6 %all-to-all-start.1 = ((bf16[128,16,2]{0,2,1:T(2,128)(2,1)}), bf16[128,16,2]{0,2,1:T(2,128)(2,1)S(1)}, u32[]{:S(2)}, u32[]{:S(2)}) async-start(bf16[128,16,2]{0,2,1:T(2,128)(2,1)} %param.15), calls=%async_computation.1 | async-start | bytes 16384 | tf_op jit(solution)/shard_map/all_to_all | solution.py:44
  11.5 8.8 copy-start.3
  16.1 19.3 %all-to-all-start = ((bf16[128,16,2,128]{3,2,0,1:T(2,128)(2,1)}), bf16[128,16,2,128]{3,2,0,1:T(2,128)(2,1)S(1)}, u32[]{:S(2)}, u32[]{:S(2)}) async-start(bf16[128,16,2,128]{3,2,0,1:T(2,128)(2,1)} %copy.61), calls=%async_computation | async-start | bytes 2097152 | tf_op jit(solution)/shard_map/all_to_all | solution.py:42
  35.4 332.1 %all-to-all-start.2 = ((bf16[128,16,2,128]{3,2,0,1:T(2,128)(2,1)}), bf16[128,16,2,128]{3,2,0,1:T(2,128)(2,1)S(1)}, u32[]{:S(2)}, u32[]{:S(2)}) async-start(bf16[128,16,2,128]{3,2,0,1:T(2,128)(2,1)} %copy.65), calls=%async_computation.2 | async-start | bytes 2097152 | tf_op jit(solution)/shard_map/all_to_all | solution.py:43
  39.7 555.1 %all-gather.5.cloned.1.call-start = ((), (), s32[]{:S(2)}) async-start(), calls=%async_computation.5 | async-start | bytes 8519680 | tf_op jit(solution)/shard_map/all_gather | solution.py:11
  368.5 1.6 copy-start.2
  384.1 60.0 %copy-start.4 = (bf16[128,16,128]{2,1,0:T(8,128)(2,1)S(1)}, bf16[128,16,128]{2,1,0:T(8,128)(2,1)}, u32[]{:S(2)}) copy-start(bf16[128,16,128]{2,1,0:T(8,128)(2,1)} %param.12) | copy-start | bytes 1572868
  442.6 0.6 copy-start.1
  442.6 0.7 copy-start
  443.3 306.3 %all-gather.7.cloned.1.call-start = ((), (), s32[]{:S(2)}) async-start(), calls=%async_computation.6 | async-start | bytes 8519680 | tf_op jit(solution)/shard_map/all_gather | solution.py:11
  445.0 14.4 %all-to-all-start.3 = ((bf16[128,16,128]{2,0,1:T(8,128)(2,1)}), bf16[128,16,128]{2,0,1:T(8,128)(2,1)}, u32[]{:S(2)}, u32[]{:S(2)}) async-start(bf16[128,16,128]{2,0,1:T(8,128)(2,1)} %copy.73), calls=%async_computation.3 | async-start | bytes 1048576 | tf_op jit(solution)/shard_map/all_to_all | solution.py:41
  811.5 75.0 %copy-start.6 = (f32[2,128]{1,0:T(2,128)S(1)}, f32[2,128]{1,0:T(2,128)}, u32[]{:S(2)}) copy-start(f32[2,128]{1,0:T(2,128)} %param.17) | copy-start | bytes 3076
  915.1 1.0 copy-start.5
Sparse Core Ops, SparseCore 0:
  443.4 151.3 all-gather.4
  597.7 151.7 all-gather.6
where the time goes:
time: 942 us; the launch traced here: 924 us
  other arithmetic  326 us (35%)
  waiting for transfers between devices  308 us (33%)
  matrix products  209 us (22%)
  blocking collectives  27.4 us (3%)
  local copies, waits for them, and re-layouts  18.7 us (2%)
  starting transfers between devices  18.3 us (2%)
  between operations  13.6 us (1%)
    another operation x2, other arithmetic, local(): lax.linalg.triangular_solve(system, right_sides, left_side=True, lower=Tr...  316 us
    all_gather x2, waiting for transfers between devices, entering(): gathered = jax.tree.map(lambda a: lax.all_gather(a, axis), part)  285 us
    dot_general x48, matrix products, compose_pair(): jnp.einsum('hkl,hlm->hkm', late_tr, early_st, precision=exact_prec)  59.5 us
    all_to_all x1, blocking collectives, local(): lax.all_to_all(jnp.transpose(normed, (1, 0, 2)), 'head', split_axis=0, co...  27.4 us
    dot_general x16, matrix products, compose_local(): jnp.einsum('hik,hkl->hil', w_group, carry_state, precision=exact_prec)  19.8 us
    dot_general x16, matrix products, group_out(): jnp.einsum('hik,hkl->hil', w_group, carry_state, precision=exact_prec)  19.8 us
    dot_general x16, matrix products, group_out(): jnp.einsum('hik,hil->hkl', keys_group, fresh_vals, precision=exact_prec)  19.1 us
    dot_general x16, matrix products, compose_local(): jnp.einsum('hkl,hlm->hkm', transit, transit_all, precision=exact_prec)  18.9 us
  transfers between devices with their start and end apart: 6, of which 5 were waited for; matrix products, arithmetic and copies ran while one was open for 37% of the time, Pallas kernels for 0%

commit v1 on v0

v1 whole, which is shorter than its diff:
```python
import functools
import jax, jax.numpy as jnp
from jax import lax
from jax.experimental import pallas as pl
from jax.experimental.pallas import tpu as pltpu
from jax.sharding import PartitionSpec as P
f32, bf16 = jnp.float32, jnp.bfloat16
D = 128
N = 256
T = 128
BASE = 16

def split(a):
    hi = a.astype(bf16)
    return hi, (a - hi.astype(f32)).astype(bf16)

def mm(a, b):
    return lax.dot_general(a, b, (((1,), (0,)), ((), ())), preferred_element_type=f32)

def mm_nt(a, b):
    return lax.dot_general(a, b, (((1,), (1,)), ((), ())), preferred_element_type=f32)

def mm_tn(a, b):
    return lax.dot_general(a, b, (((0,), (0,)), ((), ())), preferred_element_type=f32)

def dot3(a, b):
    ah, al = split(a)
    bh, bl = split(b)
    return dot3s(ah, al, bh, bl)

def dot3s(ah, al, bh, bl):
    if ah.shape[1] == 128:
        return mm(jnp.concatenate([ah, al], 1), jnp.concatenate([bh, bh], 0)) + mm(ah, bl)
    return mm(ah, bh) + (mm(al, bh) + mm(ah, bl))

def unit_lower_inverses(lows):
    n = len(lows)
    lane = lax.broadcasted_iota(jnp.int32, (BASE, 128), 1)
    row = lax.broadcasted_iota(jnp.int32, (BASE, 128), 0)
    blk = lane // BASE
    packed = []
    for low in lows:
        z = jnp.zeros((BASE, 128), f32)
        for b in range(128 // BASE):
            z = jnp.where(blk == b, low[BASE * b:BASE * (b + 1), :], z)
        packed.append(jnp.where(row > lane % BASE, z, 0.0))
    eye = jnp.where(row == lane % BASE, 1.0, 0.0).astype(f32)
    xs = [eye for _ in lows]
    for j in range(BASE - 1):
        idx = blk * BASE + j
        for i in range(n):
            lj = jnp.take_along_axis(packed[i], idx, axis=1, mode="promise_in_bounds")
            xs[i] = xs[i] - lj * xs[i][j:j + 1, :]
    fulls = []
    for x in xs:
        fulls.append(jnp.concatenate([jnp.where(blk == b, x, 0.0) for b in range(128 // BASE)], axis=0))
    m = BASE
    r2 = lax.broadcasted_iota(jnp.int32, (128, 128), 0)
    c2 = lax.broadcasted_iota(jnp.int32, (128, 128), 1)
    while m < 128:
        offmask = ((r2 // m) % 2 == 1) & (c2 // m == r2 // m - 1)
        out = []
        for i in range(n):
            x = fulls[i]
            odd = [x[m * (2 * b + 1):m * (2 * b + 2), :] for b in range(64 // m)]
            xo = jnp.concatenate(odd, 0) if len(odd) > 1 else odd[0]
            off = jnp.where(offmask, lows[i], 0.0)
            xh, xl = split(x)
            xoh, xol = split(xo)
            y = dot3s(xoh, xol, *split(off))
            z = xo - dot3s(*split(y), xh, xl)
            rows = []
            for b in range(64 // m):
                rows.append(x[m * 2 * b:m * (2 * b + 1), :])
                rows.append(z[m * b:m * (b + 1), :])
            out.append(jnp.concatenate(rows, 0))
        fulls = out
        m *= 2
    return fulls

def local_kernel(hb, k_ref, v_ref, q_ref, b_ref, ab_ref, qo_ref):
    g = pl.program_id(0)
    lane = lax.broadcasted_iota(jnp.int32, (N, 16), 1)
    betas = b_ref[...]
    r2 = lax.broadcasted_iota(jnp.int32, (128, 128), 0)
    c2 = lax.broadcasted_iota(jnp.int32, (128, 128), 1)
    vis = lax.broadcasted_iota(jnp.int32, (T, N), 1) <= 2 * lax.broadcasted_iota(jnp.int32, (T, N), 0) + 1
    eye = jnp.where(r2 == c2, 1.0, 0.0).astype(f32)
    lows, rest = [], []
    for h in range(hb):
        k = k_ref[h]
        kf = k.astype(f32)
        ssq = jnp.sum(kf * kf, axis=1, keepdims=True) + 1e-6
        beta = jnp.sum(jnp.where(lane == g * hb + h, betas, 0.0), axis=1, keepdims=True)
        p = beta / ssq
        bs = beta * lax.rsqrt(ssq)
        gram = mm_nt(k, k)
        l11 = jnp.where(r2 > c2, p[:128] * gram[:128, :128], 0.0)
        l22 = jnp.where(r2 > c2, p[128:] * gram[128:, 128:], 0.0)
        l21 = p[128:] * gram[128:, :128]
        rhs = jnp.concatenate([p * kf, bs * v_ref[h].astype(f32)], axis=1)
        lows += [l11, l22]
        rest.append((k, l21, rhs))
    invs = unit_lower_inverses(lows)
    for h in range(hb):
        k, l21, rhs = rest[h]
        t1, t2 = invs[2 * h], invs[2 * h + 1]
        y1 = dot3(t1, rhs[:128])
        y2 = dot3(t2, rhs[128:] - dot3(l21, y1))
        yh, yl = split(jnp.concatenate([y1, y2], 0))
        ky = mm_tn(k, yh) + mm_tn(k, yl)
        ab_ref[h, :, :128] = eye - ky[:, :128]
        ab_ref[h, :, 128:] = ky[:, 128:]
        q = q_ref[h]
        s = jnp.where(vis, mm_nt(q, k), 0.0)
        sh, sl = split(s)
        sy = dot3s(sh, sl, yh, yl)
        qo_ref[h, :, :128] = q.astype(f32) - sy[:, :128]
        qo_ref[h, :, 128:] = sy[:, 128:]

def local_maps(keys, values, queries, betas, hb=2):
    H = keys.shape[0]
    return pl.pallas_call(
        functools.partial(local_kernel, hb),
        grid=(H // hb,),
        in_specs=[
            pl.BlockSpec((hb, N, D), lambda i: (i, 0, 0)),
            pl.BlockSpec((hb, N, D), lambda i: (i, 0, 0)),
            pl.BlockSpec((hb, T, D), lambda i: (i, 0, 0)),
            pl.BlockSpec((N, 16), lambda i: (0, 0)),
        ],
        out_specs=[
            pl.BlockSpec((hb, D, 2 * D), lambda i: (i, 0, 0)),
            pl.BlockSpec((hb, T, 2 * D), lambda i: (i, 0, 0)),
        ],
        out_shape=[jax.ShapeDtypeStruct((H, D, 2 * D), f32), jax.ShapeDtypeStruct((H, T, 2 * D), f32)],
        compiler_params=pltpu.CompilerParams(vmem_limit_bytes=48 * 2**20),
    )(keys, values, queries, betas)

MESH = pl.DeviceIdType.MESH
HEADS = 16
NX, NL, NG, NY = 4, 4, 4, 4


def compose(late, early):
    joined = dot3(late[:, :D], early)
    return jnp.concatenate([joined[:, :D], joined[:, D:] + late[:, D:]], axis=1)


def advance(pair, state):
    return dot3(pair[:, :D], state) + pair[:, D:]


def scan_kernel(
    ab_ref, gain_ref, m_ref, gains_ref,
    both, chip, row_in, row_pre, row_tot, low_in, low_pre, low_tot,
    high_in, high_pre, high_tot, y_in, y_state, state, low_out, low_state,
    row_out, chip_state, after,
    local_sem, send, recv,
):
    seq, head = lax.axis_index("seq"), lax.axis_index("head")
    x, c = head // 2, head % 2
    y, g, l = seq // (NG * NL), (seq // NL) % NG, seq % NL
    oc = 1 - c

    def device(xx=None, cc=None, yy=None, gg=None, ll=None):
        xx, cc = x if xx is None else xx, c if cc is None else cc
        yy, gg, ll = y if yy is None else yy, g if gg is None else gg, l if ll is None else ll
        return {"seq": (yy * NG + gg) * NL + ll, "head": xx * 2 + cc}

    partner = device(cc=oc)

    def others(me, count):
        return [(me + k) % count for k in range(1, count)]

    def remote(src, dst, s, r, where):
        return pltpu.make_async_remote_copy(
            src_ref=src, dst_ref=dst, send_sem=send.at[s], recv_sem=recv.at[r],
            device_id=where, device_id_type=MESH,
        )

    peers = [partner]
    peers += [device(xx=v) for v in others(x, NX)]
    peers += [device(ll=v) for v in others(l, NL)]
    peers += [device(gg=v) for v in others(g, NG)]
    peers += [device(yy=v) for v in others(y, NY)]
    barrier = pltpu.get_barrier_semaphore()
    for peer in peers:
        pl.semaphore_signal(barrier, inc=1, device_id=peer, device_id_type=MESH)
    own = pltpu.make_async_copy(ab_ref.at[pl.ds(8 * c, 8)], both.at[c], local_sem)
    own.start()
    gains_ref[head] = gain_ref[...]
    pl.semaphore_wait(barrier, len(peers))

    pair_copies = []
    for i in range(8):
        copy = remote(ab_ref.at[8 * oc + i], both.at[c, i], i, i, partner)
        copy.start()
        pair_copies.append(copy)
    gain_copy = remote(gain_ref, gains_ref.at[head], 8, 8, partner)
    gain_copy.start()
    own.wait()

    def pair_recv(i):
        remote(ab_ref.at[i], both.at[oc, i], i, i, partner).wait_recv()

    row_copies = []
    for k in (1, 2, 3, 0):
        dest = (x + k) % NX
        for e in range(2):
            i = 2 * dest + e
            remote(ab_ref.at[i], both.at[oc, i], i, i, partner).wait_recv()
            joined = compose(both[1, i], both[0, i])
            if k == 0:
                row_in[x, e] = joined
            else:
                chip[i] = joined
        if k:
            copy = remote(chip.at[pl.ds(2 * dest, 2)], row_in.at[x], 9 + k, 9 + x, device(xx=dest))
            copy.start()
            row_copies.append(copy)
    remote(gain_ref, gains_ref.at[2 * x + oc], 8, 8, partner).wait_recv()
    gain_copies = []
    for k in (1, 2, 3):
        copy = remote(
            gains_ref.at[pl.ds(2 * x, 2)], gains_ref.at[pl.ds(2 * x, 2)], 13 + k, 13 + x,
            device(xx=(x + k) % NX),
        )
        copy.start()
        gain_copies.append(copy)

    for k in (1, 2, 3):
        origin = (x + k) % NX
        remote(chip.at[pl.ds(0, 2)], row_in.at[origin], 9 + k, 9 + origin, device(xx=origin)).wait_recv()
    for e in range(2):
        row_pre[0, e] = row_in[0, e]
    for s in (1, 2):
        for e in range(2):
            row_pre[s, e] = compose(row_in[s, e], row_pre[s - 1, e])
    for e in range(2):
        row_tot[e] = compose(row_in[3, e], row_pre[2, e])

    active = l % 2 == c
    for e in range(2):
        owner = 2 * e + c
        out = remote(row_tot.at[e], low_in.at[l], 17 + e, 17 + l, device(ll=owner))

        @pl.when(owner != l)
        def _():
            out.start()

        @pl.when(owner == l)
        def _():
            low_in[l] = row_tot[e]

    def high_copy(k, there, slot):
        return remote(high_tot, high_in.at[slot], 21 + k, 21 + slot, device(gg=there))

    def y_copy(k, there, slot):
        return remote(low_tot, y_in.at[slot], 25 + k, 25 + slot, device(yy=there))

    def low_copy(k, there, e):
        return remote(low_out.at[there], low_state.at[e], 29 + k, 29 + e, device(ll=there))

    @pl.when(active)
    def _():
        for k in (1, 2, 3):
            origin = (l + k) % NL
            remote(row_tot.at[0], low_in.at[origin], 17, 17 + origin, device(ll=origin)).wait_recv()
        low_pre[0] = low_in[0]
        for s in (1, 2):
            low_pre[s] = compose(low_in[s], low_pre[s - 1])
        total = compose(low_in[3], low_pre[2])
        high_tot[...] = total
        high_in[g] = total
        for k in (1, 2, 3):
            high_copy(k, (g + k) % NG, g).start()
        for k in (1, 2, 3):
            origin = (g + k) % NG
            high_copy(k, origin, origin).wait_recv()
        high_pre[0] = high_in[0]
        for s in (1, 2):
            high_pre[s] = compose(high_in[s], high_pre[s - 1])
        total = compose(high_in[3], high_pre[2])
        low_tot[...] = total
        y_in[y] = total
        for k in (1, 2, 3):
            y_copy(k, (y + k) % NY, y).start()
        for k in (1, 2, 3):
            origin = (y + k) % NY
            y_copy(k, origin, origin).wait_recv()
        y_state[0] = jnp.zeros((D, D), f32)
        y_state[1] = y_in[0, :, D:]
        for s in (1, 2):
            y_state[s + 1] = advance(y_in[s], y_state[s])
        state[...] = y_state[y]

        @pl.when(g > 0)
        def _():
            state[...] = advance(high_pre[g - 1], state[...])

        low_out[0] = state[...]
        for s in (0, 1, 2):
            low_out[s + 1] = advance(low_pre[s], state[...])
        for k in (1, 2, 3):
            low_copy(k, (l + k) % NL, l // 2).start()
        low_state[l // 2] = low_out[l]

    for e in range(2):
        owner = 2 * e + c

        @pl.when(owner != l)
        def _():
            low_copy(0, owner, e).wait_recv()

    for e in range(2):
        row_out[0, e] = low_state[e]
        for s in (0, 1, 2):
            row_out[s + 1, e] = advance(row_pre[s, e], low_state[e])
    state_copies = []
    for k in (1, 2, 3):
        dest = (x + k) % NX
        copy = remote(row_out.at[dest], chip_state.at[pl.ds(2 * x, 2)], 33 + k, 33 + x, device(xx=dest))
        copy.start()
        state_copies.append(copy)
    for e in range(2):
        chip_state[2 * x + e] = row_out[x, e]

    def back_copy(i):
        return remote(after.at[i], m_ref.at[8 * c + i], 37 + i, 37 + i, partner)

    for k in (0, 1, 2, 3):
        origin = (x + k) % NX
        if k:
            remote(
                row_out.at[origin], chip_state.at[pl.ds(2 * origin, 2)], 33 + k, 33 + origin, device(xx=origin)
            ).wait_recv()
        for e in range(2):
            i = 2 * origin + e
            begin = chip_state[i]
            end = advance(both[0, i], begin)

            @pl.when(c == 0)
            def _():
                m_ref[i] = begin
                after[i] = end

            @pl.when(c == 1)
            def _():
                m_ref[8 + i] = end
                after[i] = begin

            back_copy(i).start()
    for i in range(8):
        remote(after.at[i], m_ref.at[8 * oc + i], 37 + i, 37 + i, partner).wait_recv()
    for k in (1, 2, 3):
        origin = (x + k) % NX
        remote(
            gains_ref.at[pl.ds(2 * origin, 2)], gains_ref.at[pl.ds(2 * origin, 2)], 13 + k, 13 + origin,
            device(xx=origin),
        ).wait_recv()

    for copy in pair_copies + [gain_copy] + row_copies + gain_copies + state_copies:
        copy.wait_send()
    for e in range(2):
        @pl.when(2 * e + c != l)
        def _():
            remote(row_tot.at[e], low_in.at[l], 17 + e, 17 + l, device(ll=2 * e + c)).wait_send()

    @pl.when(active)
    def _():
        for k in (1, 2, 3):
            high_copy(k, (g + k) % NG, g).wait_send()
            y_copy(k, (y + k) % NY, y).wait_send()
            low_copy(k, (l + k) % NL, l // 2).wait_send()
    for i in range(8):
        back_copy(i).wait_send()


def scan_states(ab, gain):
    wide, square = (D, 2 * D), (D, D)
    vm = lambda *s: pltpu.VMEM(s, f32)
    return pl.pallas_call(
        scan_kernel,
        in_specs=[pl.BlockSpec(memory_space=pltpu.VMEM), pl.BlockSpec(memory_space=pltpu.VMEM)],
        out_specs=[pl.BlockSpec(memory_space=pltpu.VMEM), pl.BlockSpec(memory_space=pltpu.VMEM)],
        out_shape=[jax.ShapeDtypeStruct((HEADS, D, D), f32), jax.ShapeDtypeStruct((8, 8, D), f32)],
        scratch_shapes=[
            vm(2, 8, *wide), vm(8, *wide), vm(NX, 2, *wide), vm(NX, 2, *wide), vm(2, *wide),
            vm(NL, *wide), vm(NL, *wide), vm(*wide),
            vm(NG, *wide), vm(NG, *wide), vm(*wide), vm(NY, *wide), vm(NY, *square), vm(*square),
            vm(NL, *square), vm(2, *square),
            vm(NX, 2, *square), vm(8, *square), vm(8, *square),
            pltpu.SemaphoreType.DMA, pltpu.SemaphoreType.DMA((45,)), pltpu.SemaphoreType.DMA((45,)),
        ],
        compiler_params=pltpu.CompilerParams(
            collective_id=0, has_side_effects=True, vmem_limit_bytes=48 * 2**20
        ),
    )(ab, gain)


def output_kernel(qo_ref, m_ref, gains_ref, gate_ref, out_ref, rows):
    for h in range(HEADS):
        r = dot3(qo_ref[h, :, :D], m_ref[h]) + qo_ref[h, :, D:]
        scale = lax.rsqrt(jnp.mean(r * r, axis=-1, keepdims=True) + 1e-6)
        rows[h] = r * scale * gains_ref[h // 2, h % 2 : h % 2 + 1, :]
    gate = gate_ref[...].astype(f32)
    normed = jnp.swapaxes(rows[...], 0, 1)
    out_ref[...] = (normed * (gate / (1.0 + jnp.exp(-gate)))).astype(bf16)


def outputs(qo, m, gains, gate):
    whole = pl.BlockSpec(memory_space=pltpu.VMEM)
    return pl.pallas_call(
        output_kernel,
        in_specs=[whole] * 4,
        out_specs=whole,
        out_shape=jax.ShapeDtypeStruct((T, HEADS, D), bf16),
        scratch_shapes=[pltpu.VMEM((HEADS, T, D), f32)],
        compiler_params=pltpu.CompilerParams(vmem_limit_bytes=48 * 2**20),
    )(qo, m, gains, gate)


def local(queries, keys, values, betas, gate, gain):
    keys_h = jnp.transpose(keys, (1, 0, 2, 3)).reshape(HEADS, N, D)
    values_h = jnp.transpose(values, (1, 0, 2, 3)).reshape(HEADS, N, D)
    queries_h = jnp.transpose(queries, (1, 0, 2))
    betas_h = jnp.transpose(betas, (0, 2, 1)).reshape(N, HEADS).astype(f32)
    ab, qo = local_maps(keys_h, values_h, queries_h, betas_h)
    m, gains = scan_states(ab, jnp.pad(gain, ((0, 6), (0, 0))))
    return outputs(qo, m, gains, gate)


def solution(mesh):
    return jax.shard_map(
        local,
        mesh=mesh,
        in_specs=(
            P(("seq", "head"), None, None),
            P(("seq", "head"), None, None, None),
            P(("seq", "head"), None, None, None),
            P(("seq", "head"), None, None),
            P(("seq", "head"), None, None),
            P("head", None),
        ),
        out_specs=P(("seq", "head"), None, None),
        check_vma=False,
    )
```

time: 942 us -> 112 us (0.12)
  the two profiles are of different devices: /device:TPU:25 before, /device:TPU:1 now
where the time goes in v1:
time: 112 us
  Pallas kernels  108 us (96%)
  local copies, waits for them, and re-layouts  3.55 us (3%)
    pallas_call x1, Pallas kernels, scan_states(): pl.pallas_call(scan_kernel, in_specs=[pl.BlockSpec(memory_space=pltpu.VME...  76.8 us
    pallas_call x1, Pallas kernels, local_maps(): pl.pallas_call(functools.partial(local_kernel, hb), grid=(H // hb,), in_s...  29.7 us
    transpose x1, local copies, waits for them, and re-layouts, local(): keys_h = jnp.transpose(keys, (1, 0, 2, 3)).reshape(HEADS, N, D)  2.3 us

profile of v1, /device:TPU:1, one launch (start us, length us, event | category | flops | bytes accessed | tf_op | source)
XLA Modules:
  0.0 112.1 jit_solution(7692867543495770123)
XLA Ops:
  0.0 0.0 copy-start.2
  0.0 0.0 copy-start.3
  0.0 2.3 %copy.7 = bf16[16,128,2,128]{3,2,1,0:T(2,128)(2,1)S(1)} copy(bf16[16,128,2,128]{3,2,0,1:T(2,128)(2,1)} %bitcast.14) | data formatting | bytes 2097152 | tf_op jit(solution)/shard_map/transpose | solution.py:425
  2.3 0.0 copy-start.4
  2.3 0.0 copy-done.2
  2.3 1.0 copy.8
  3.3 0.0 copy-start.5
  3.3 0.0 copy-done.3
  3.3 0.1 copy.12
  3.5 0.0 copy-done.4
  3.5 0.1 copy.10
  3.6 0.0 copy-start.1
  3.6 29.7 %shard_map.64 = (f32[16,128,256]{2,1,0:T(8,128)S(1)}, f32[16,128,256]{2,1,0:T(8,128)}) custom-call(bf16[16,256,128]{2,1,0:T(8,128)(2,1)S(1)} %bitcast.10, bf16[16,256,128]{2,1,0:T(8,128)(2,1)S(1)} %bitcast.11, bf16[16,128,128]{2,1,0:T(8,128)(2,1)S(1)} %bitcast.12, f32[256,16]{1,0:T(8,128)S(1)} %bitcast.13), custom_call_target="tpu_custom_call" | custom-call | tf_op jit(solution)/shard_map/pallas_call | solution.py:123
  33.3 0.0 copy-start
  33.3 0.0 copy-done.5
  33.3 76.8 %shard_map.65 = (f32[16,128,128]{2,1,0:T(8,128)S(1)}, f32[8,8,128]{2,1,0:T(8,128)S(1)}) custom-call(f32[16,128,256]{2,1,0:T(8,128)S(1)} %get-tuple-element.10.ab_ref, f32[8,128]{1,0:T(8,128)S(1)} %pad.4.gain_ref), custom_call_target="tpu_custom_call" | custom-call | tf_op jit(solution)/shard_map/pallas_call | solution.py:383
  110.1 0.0 copy-done.1
  110.1 0.0 copy-done
  110.1 2.0 %shard_map.66 = bf16[128,16,128]{2,1,0:T(8,128)(2,1)} custom-call(f32[16,128,256]{2,1,0:T(8,128)S(1)} %copy-done, f32[16,128,128]{2,1,0:T(8,128)S(1)} %get-tuple-element.11.m_ref, f32[8,8,128]{2,1,0:T(8,128)S(1)} %get-tuple-element.12.gains_ref, bf16[128,16,128]{2,1,0:T(8,128)(2,1)S(1)} %copy-done.1), custom_call_target="tpu_custom_call" | custom-call | tf_op jit(solution)/shard_map/pallas_call | solution.py:414
  (2 shorter events, 0.0 us)
Async XLA Ops:
  0.0 2.3 %copy-start.2 = (bf16[128,16,2,128]{3,2,1,0:T(2,128)(2,1)S(1)}, bf16[128,16,2,128]{3,2,1,0:T(2,128)(2,1)}, u32[]{:S(2)}) copy-start(bf16[128,16,2,128]{3,2,1,0:T(2,128)(2,1)} %param.8) | copy-start | bytes 3145732
  0.0 3.3 %copy-start.3 = (bf16[128,16,128]{2,1,0:T(8,128)(2,1)S(1)}, bf16[128,16,128]{2,1,0:T(8,128)(2,1)}, u32[]{:S(2)}) copy-start(bf16[128,16,128]{2,1,0:T(8,128)(2,1)} %param.6) | copy-start | bytes 1572868
  2.3 1.2 %copy-start.4 = (bf16[128,16,2]{0,2,1:T(2,128)(2,1)S(1)}, bf16[128,16,2]{0,2,1:T(2,128)(2,1)}, u32[]{:S(2)}) copy-start(bf16[128,16,2]{0,2,1:T(2,128)(2,1)} %param.9) | copy-start | bytes 24580
  3.3 30.0 %copy-start.5 = (f32[2,128]{1,0:T(2,128)S(1)}, f32[2,128]{1,0:T(2,128)}, u32[]{:S(2)}) copy-start(f32[2,128]{1,0:T(2,128)} %param.11) | copy-start | bytes 3076
  3.6 106.5 %copy-start.1 = (bf16[128,16,128]{2,1,0:T(8,128)(2,1)S(1)}, bf16[128,16,128]{2,1,0:T(8,128)(2,1)}, u32[]{:S(2)}) copy-start(bf16[128,16,128]{2,1,0:T(8,128)(2,1)} %gate_ref.1) | copy-start | bytes 1572868
  33.3 76.8 %copy-start = (f32[16,128,256]{2,1,0:T(8,128)S(1)}, f32[16,128,256]{2,1,0:T(8,128)}, u32[]{:S(2)}) copy-start(f32[16,128,256]{2,1,0:T(8,128)} %get-tuple-element.9.qo_ref) | copy-start | bytes 6291460

commit v2 on v1

v2 whole, which is shorter than its diff:
```python
import functools
import jax, jax.numpy as jnp
from jax import lax
from jax.experimental import pallas as pl
from jax.experimental.pallas import tpu as pltpu
from jax.sharding import PartitionSpec as P
f32, bf16 = jnp.float32, jnp.bfloat16
D = 128
N = 256
T = 128
BASE = 16

def split(a):
    hi = a.astype(bf16)
    return hi, (a - hi.astype(f32)).astype(bf16)

def mm(a, b):
    return lax.dot_general(a, b, (((1,), (0,)), ((), ())), preferred_element_type=f32)

def mm_nt(a, b):
    return lax.dot_general(a, b, (((1,), (1,)), ((), ())), preferred_element_type=f32)

def mm_tn(a, b):
    return lax.dot_general(a, b, (((0,), (0,)), ((), ())), preferred_element_type=f32)

def dot3(a, b):
    ah, al = split(a)
    bh, bl = split(b)
    return dot3s(ah, al, bh, bl)

def dot3s(ah, al, bh, bl):
    if ah.shape[1] == 128:
        return mm(jnp.concatenate([ah, al], 1), jnp.concatenate([bh, bh], 0)) + mm(ah, bl)
    return mm(ah, bh) + (mm(al, bh) + mm(ah, bl))

def unit_lower_inverses(lows):
    n = len(lows)
    lane = lax.broadcasted_iota(jnp.int32, (BASE, 128), 1)
    row = lax.broadcasted_iota(jnp.int32, (BASE, 128), 0)
    blk = lane // BASE
    packed = []
    for low in lows:
        z = jnp.zeros((BASE, 128), f32)
        for b in range(128 // BASE):
            z = jnp.where(blk == b, low[BASE * b:BASE * (b + 1), :], z)
        packed.append(jnp.where(row > lane % BASE, z, 0.0))
    eye = jnp.where(row == lane % BASE, 1.0, 0.0).astype(f32)
    xs = [eye for _ in lows]
    for j in range(BASE - 1):
        idx = blk * BASE + j
        for i in range(n):
            lj = jnp.take_along_axis(packed[i], idx, axis=1, mode="promise_in_bounds")
            xs[i] = xs[i] - lj * xs[i][j:j + 1, :]
    fulls = []
    for x in xs:
        fulls.append(jnp.concatenate([jnp.where(blk == b, x, 0.0) for b in range(128 // BASE)], axis=0))
    m = BASE
    r2 = lax.broadcasted_iota(jnp.int32, (128, 128), 0)
    c2 = lax.broadcasted_iota(jnp.int32, (128, 128), 1)
    while m < 128:
        offmask = ((r2 // m) % 2 == 1) & (c2 // m == r2 // m - 1)
        out = []
        for i in range(n):
            x = fulls[i]
            odd = [x[m * (2 * b + 1):m * (2 * b + 2), :] for b in range(64 // m)]
            xo = jnp.concatenate(odd, 0) if len(odd) > 1 else odd[0]
            off = jnp.where(offmask, lows[i], 0.0)
            xh, xl = split(x)
            xoh, xol = split(xo)
            y = dot3s(xoh, xol, *split(off))
            z = xo - dot3s(*split(y), xh, xl)
            rows = []
            for b in range(64 // m):
                rows.append(x[m * 2 * b:m * (2 * b + 1), :])
                rows.append(z[m * b:m * (b + 1), :])
            out.append(jnp.concatenate(rows, 0))
        fulls = out
        m *= 2
    return fulls

MESH = pl.DeviceIdType.MESH
HEADS = 16
NX, NL, NG, NY = 4, 4, 4, 4
PAIR, ROW, LOW, HIGH, YS, HIGH_BACK, LOW_BACK, ROW_BACK, BACK, GAIN, GAIN_ROW, SEMS = (
    0, 8, 16, 24, 32, 40, 48, 56, 64, 72, 73, 77,
)


def local_maps(keys, values, queries, betas):
    r2 = lax.broadcasted_iota(jnp.int32, (128, 128), 0)
    c2 = lax.broadcasted_iota(jnp.int32, (128, 128), 1)
    vis = lax.broadcasted_iota(jnp.int32, (T, N), 1) <= 2 * lax.broadcasted_iota(jnp.int32, (T, N), 0) + 1
    eye = jnp.where(r2 == c2, 1.0, 0.0).astype(f32)
    lows, rest = [], []
    for k, v, beta in zip(keys, values, betas):
        kf = k.astype(f32)
        ssq = jnp.sum(kf * kf, axis=1, keepdims=True) + 1e-6
        p = beta / ssq
        bs = beta * lax.rsqrt(ssq)
        gram = mm_nt(k, k)
        l11 = jnp.where(r2 > c2, p[:128] * gram[:128, :128], 0.0)
        l22 = jnp.where(r2 > c2, p[128:] * gram[128:, 128:], 0.0)
        l21 = p[128:] * gram[128:, :128]
        rhs = jnp.concatenate([p * kf, bs * v.astype(f32)], axis=1)
        lows += [l11, l22]
        rest.append((l21, rhs))
    invs = unit_lower_inverses(lows)
    maps, outs = [], []
    for h, (k, q) in enumerate(zip(keys, queries)):
        l21, rhs = rest[h]
        t1, t2 = invs[2 * h], invs[2 * h + 1]
        y1 = dot3(t1, rhs[:128])
        y2 = dot3(t2, rhs[128:] - dot3(l21, y1))
        yh, yl = split(jnp.concatenate([y1, y2], 0))
        ky = mm_tn(k, yh) + mm_tn(k, yl)
        maps.append((eye - ky[:, :128], ky[:, 128:]))
        s = jnp.where(vis, mm_nt(q, k), 0.0)
        sh, sl = split(s)
        sy = dot3s(sh, sl, yh, yl)
        outs.append((q.astype(f32) - sy[:, :128], sy[:, 128:]))
    return maps, outs


def compose(late, early):
    joined = dot3(late[:, :D], early)
    return jnp.concatenate([joined[:, :D], joined[:, D:] + late[:, D:]], axis=1)


def advance(pair, state):
    return dot3(pair[:, :D], state) + pair[:, D:]


def states_kernel(
    k_ref, v_ref, q_ref, b_ref, gain_ref, qo_ref, m_ref, gains_ref,
    outbox, both, chip, row_in, row_pre, row_tot, low_in, low_pre, low_tot,
    high_in, high_pre, high_tot, y_in, y_state, high_out, high_state, low_out, low_state,
    row_out, chip_state, after, send, recv,
):
    seq, head = lax.axis_index("seq"), lax.axis_index("head")
    x, c = head // 2, head % 2
    y, g, l = seq // (NG * NL), (seq // NL) % NG, seq % NL
    oc = 1 - c

    def device(xx=None, cc=None, yy=None, gg=None, ll=None):
        xx, cc = x if xx is None else xx, c if cc is None else cc
        yy, gg, ll = y if yy is None else yy, g if gg is None else gg, l if ll is None else ll
        return {"seq": (yy * NG + gg) * NL + ll, "head": xx * 2 + cc}

    partner = device(cc=oc)

    def remote(src, dst, s, r, where):
        return pltpu.make_async_remote_copy(
            src_ref=src, dst_ref=dst, send_sem=send.at[s], recv_sem=recv.at[r],
            device_id=where, device_id_type=MESH,
        )

    peers = [partner]
    peers += [device(xx=(x + k) % NX) for k in (1, 2, 3)]
    peers += [device(ll=(l + k) % NL) for k in (1, 2, 3)]
    peers += [device(gg=(g + k) % NG) for k in (1, 2, 3)]
    peers += [device(yy=(y + k) % NY) for k in (1, 2, 3)]
    barrier = pltpu.get_barrier_semaphore()
    for peer in peers:
        pl.semaphore_signal(barrier, inc=1, device_id=peer, device_id_type=MESH)
    gains_ref[head] = gain_ref[...]
    pl.semaphore_wait(barrier, len(peers))

    def gain_copy():
        return remote(gain_ref, gains_ref.at[head], GAIN, GAIN, partner)

    def gain_row_copy(k, there, origin):
        rows = gains_ref.at[pl.ds(2 * origin, 2)]
        return remote(rows, rows, GAIN_ROW + k, GAIN_ROW + origin, device(xx=there))

    gain_copy().start()

    def pair_copy(i):
        return remote(outbox.at[i], both.at[c, i], PAIR + i, PAIR + i, partner)

    def pair_wait(i):
        remote(outbox.at[i], both.at[oc, i], PAIR + i, PAIR + i, partner).wait_recv()

    def row_copy(e, k, there, origin):
        return remote(
            chip.at[2 * there + e], row_in.at[e, origin], ROW + 4 * e + k, ROW + 4 * e + origin, device(xx=there)
        )

    def low_copy(e, there, origin):
        return remote(row_tot.at[e], low_in.at[e, origin], LOW + 4 * e, LOW + 4 * e + origin, device(ll=there))

    def high_copy(e, there, origin):
        return remote(low_tot.at[e], high_in.at[e, origin], HIGH + 4 * e, HIGH + 4 * e + origin, device(gg=there))

    def y_copy(e, k, there, origin):
        return remote(high_tot.at[e], y_in.at[e, origin], YS + 4 * e + k, YS + 4 * e + origin, device(yy=there))

    def high_back(e, there):
        return remote(
            high_out.at[e, there], high_state.at[e], HIGH_BACK + 4 * e + there, HIGH_BACK + 4 * e, device(gg=there)
        )

    def low_back(e, there):
        return remote(
            low_out.at[e, there], low_state.at[e], LOW_BACK + 4 * e + there, LOW_BACK + 4 * e, device(ll=there)
        )

    def row_back(e, k, there, origin):
        return remote(
            row_out.at[e, there], chip_state.at[2 * origin + e], ROW_BACK + 4 * e + k, ROW_BACK + 4 * e + origin,
            device(xx=there),
        )

    def back_copy(i):
        return remote(after.at[i], m_ref.at[8 * c + i], BACK + i, BACK + i, partner)

    def back_wait(i):
        remote(after.at[i], m_ref.at[8 * oc + i], BACK + i, BACK + i, partner).wait_recv()

    def joint(parts, e, pre, tot):
        first = compose(parts[e, 1], parts[e, 0])
        last = compose(parts[e, 3], parts[e, 2])
        tot[e] = compose(last, first)
        pre[e, 0] = first

    def third(parts, e, pre):
        pre[e, 1] = compose(parts[e, 2], pre[e, 0])

    def prefix(parts, pre, e, place):
        return parts[e, 0] if place == 1 else pre[e, place - 2]

    def join_chip(it):
        e, s = it // 4, it % 4
        there = (x + 1 + s) % NX
        i = 2 * there + e
        pair_wait(i)
        joined = compose(both[1, i], both[0, i])

        @pl.when(s < 3)
        def _():
            chip[i] = joined
            row_copy(e, 1 + s, there, x).start()

        @pl.when(s == 3)
        def _():
            row_in[e, x] = joined

    def up_row(e):
        own = 2 * e + c
        for k in (1, 2, 3):
            origin = (x + k) % NX
            row_copy(e, 0, origin, origin).wait_recv()
        joint(row_in, e, row_pre, row_tot)

        @pl.when(l != own)
        def _():
            low_copy(e, own, l).start()

        @pl.when(l == own)
        def _():
            low_in[e, l] = row_tot[e]

        third(row_in, e, row_pre)

    def up_low(e):
        own = 2 * e + c

        @pl.when(l == own)
        def _():
            for k in (1, 2, 3):
                origin = (l + k) % NL
                low_copy(e, origin, origin).wait_recv()
            joint(low_in, e, low_pre, low_tot)

            @pl.when(g != own)
            def _():
                high_copy(e, own, g).start()

            @pl.when(g == own)
            def _():
                high_in[e, g] = low_tot[e]

            third(low_in, e, low_pre)

    def up_high(e):
        own = 2 * e + c

        @pl.when((l == own) & (g == own))
        def _():
            for k in (1, 2, 3):
                origin = (g + k) % NG
                high_copy(e, origin, origin).wait_recv()
            joint(high_in, e, high_pre, high_tot)
            for k in (1, 2, 3):
                @pl.when(y + k < NY)
                def _():
                    y_copy(e, k, (y + k) % NY, y).start()
            third(high_in, e, high_pre)

    def down_high(e):
        own = 2 * e + c

        @pl.when((l == own) & (g == own))
        def _():
            y_state[e] = jnp.zeros((D, D), f32)
            for s in (0, 1, 2):
                @pl.when(y > s)
                def _():
                    y_copy(e, 0, s, s).wait_recv()
                    y_state[e] = advance(y_in[e, s], y_state[e])
            start = y_state[e]
            for place in range(NG):
                high_out[e, place] = start if place == 0 else advance(prefix(high_in, high_pre, e, place), start)

                @pl.when(g != place)
                def _():
                    high_back(e, place).start()

                @pl.when(g == place)
                def _():
                    high_state[e] = high_out[e, place]

    def down_low(e):
        own = 2 * e + c

        @pl.when(l == own)
        def _():
            @pl.when(g != own)
            def _():
                high_back(e, own).wait_recv()
            start = high_state[e]
            for place in range(NL):
                low_out[e, place] = start if place == 0 else advance(prefix(low_in, low_pre, e, place), start)

                @pl.when(l != place)
                def _():
                    low_back(e, place).start()

                @pl.when(l == place)
                def _():
                    low_state[e] = low_out[e, place]

    def down_row(e):
        own = 2 * e + c

        @pl.when(l != own)
        def _():
            low_back(e, own).wait_recv()
        start = low_state[e]
        for place in range(NX):
            row_out[e, place] = start if place == 0 else advance(prefix(row_in, row_pre, e, place), start)
        for k in (2, 1, 3):
            row_back(e, k, (x + k) % NX, x).start()
        chip_state[2 * x + e] = row_out[e, x]

    def down_chip(e):
        for k in (0, 1, 3, 2):
            origin = (x + k) % NX
            if k:
                row_back(e, 0, origin, origin).wait_recv()
            i = 2 * origin + e
            begin = chip_state[i]
            end = advance(both[0, i], begin)

            @pl.when(c == 0)
            def _():
                m_ref[i] = begin
                after[i] = end

            @pl.when(c == 1)
            def _():
                m_ref[8 + i] = end
                after[i] = begin

            back_copy(i).start()

    lane = lax.broadcasted_iota(jnp.int32, (N, HEADS), 1)

    def turn(it, carry):
        e, s = it // 4, it % 4
        i = 2 * ((x + 1 + s) % NX) + e
        here = (8 * oc + i, 8 * c + i)
        betas = [jnp.sum(jnp.where(lane == h, b_ref[...], 0.0), axis=1, keepdims=True) for h in here]
        maps, outs = local_maps(
            [k_ref[h] for h in here], [v_ref[h] for h in here], [q_ref[h] for h in here], betas
        )
        outbox[i, :, :D], outbox[i, :, D:] = maps[0]
        pair_copy(i).start()
        both[c, i, :, :D], both[c, i, :, D:] = maps[1]
        for h, (q_part, o_part) in zip(here, outs):
            qo_ref[h, :, :D] = q_part
            qo_ref[h, :, D:] = o_part

        @pl.when(it > 0)
        def _():
            join_chip(it - 1)

        @pl.when(it == 4)
        def _():
            up_row(0)

        @pl.when(it == 5)
        def _():
            up_low(0)

        @pl.when(it == 6)
        def _():
            up_high(0)

        @pl.when(it == 7)
        def _():
            down_high(0)

        return carry

    lax.fori_loop(0, 8, turn, 0)
    join_chip(7)
    remote(gain_ref, gains_ref.at[2 * x + oc], GAIN, GAIN, partner).wait_recv()
    for k in (1, 2, 3):
        gain_row_copy(k, (x + k) % NX, x).start()
    up_row(1)
    down_low(0)
    up_low(1)
    down_row(0)
    up_high(1)
    down_chip(0)
    down_high(1)
    down_low(1)
    down_row(1)
    down_chip(1)
    for i in range(8):
        back_wait(i)
    for k in (1, 2, 3):
        origin = (x + k) % NX
        gain_row_copy(k, origin, origin).wait_recv()

    gain_copy().wait_send()
    for k in (1, 2, 3):
        gain_row_copy(k, (x + k) % NX, x).wait_send()
    for i in range(8):
        pair_copy(i).wait_send()
        back_copy(i).wait_send()
    for e in range(2):
        own = 2 * e + c
        for k in (1, 2, 3):
            row_copy(e, k, (x + k) % NX, x).wait_send()
            row_back(e, k, (x + k) % NX, x).wait_send()

        @pl.when(l != own)
        def _():
            low_copy(e, own, l).wait_send()

        @pl.when(l == own)
        def _():
            @pl.when(g != own)
            def _():
                high_copy(e, own, g).wait_send()

            for place in range(NL):
                @pl.when(l != place)
                def _():
                    low_back(e, place).wait_send()

            @pl.when(g == own)
            def _():
                for k in (1, 2, 3):
                    @pl.when(y + k < NY)
                    def _():
                        y_copy(e, k, (y + k) % NY, y).wait_send()
                for place in range(NG):
                    @pl.when(g != place)
                    def _():
                        high_back(e, place).wait_send()


def states(keys, values, queries, betas, gain):
    wide, square = (D, 2 * D), (D, D)
    whole = pl.BlockSpec(memory_space=pltpu.VMEM)

    def vm(*shape):
        return pltpu.VMEM(shape, f32)

    return pl.pallas_call(
        states_kernel,
        in_specs=[whole] * 5,
        out_specs=[whole] * 3,
        out_shape=[
            jax.ShapeDtypeStruct((HEADS, T, 2 * D), f32),
            jax.ShapeDtypeStruct((HEADS, D, D), f32),
            jax.ShapeDtypeStruct((8, 8, D), f32),
        ],
        scratch_shapes=[
            vm(8, *wide), vm(2, 8, *wide), vm(8, *wide),
            vm(2, NX, *wide), vm(2, 2, *wide), vm(2, *wide),
            vm(2, NL, *wide), vm(2, 2, *wide), vm(2, *wide),
            vm(2, NG, *wide), vm(2, 2, *wide), vm(2, *wide),
            vm(2, NY, *wide), vm(2, *square),
            vm(2, NG, *square), vm(2, *square), vm(2, NL, *square), vm(2, *square),
            vm(2, NX, *square), vm(8, *square), vm(8, *square),
            pltpu.SemaphoreType.DMA((SEMS,)), pltpu.SemaphoreType.DMA((SEMS,)),
        ],
        compiler_params=pltpu.CompilerParams(
            collective_id=0, has_side_effects=True, vmem_limit_bytes=48 * 2**20
        ),
    )(keys, values, queries, betas, gain)


def output_kernel(qo_ref, m_ref, gains_ref, gate_ref, out_ref, rows):
    for h in range(HEADS):
        r = dot3(qo_ref[h, :, :D], m_ref[h]) + qo_ref[h, :, D:]
        scale = lax.rsqrt(jnp.mean(r * r, axis=-1, keepdims=True) + 1e-6)
        rows[h] = r * scale * gains_ref[h // 2, h % 2 : h % 2 + 1, :]
    gate = gate_ref[...].astype(f32)
    normed = jnp.swapaxes(rows[...], 0, 1)
    out_ref[...] = (normed * (gate / (1.0 + jnp.exp(-gate)))).astype(bf16)


def outputs(qo, m, gains, gate):
    whole = pl.BlockSpec(memory_space=pltpu.VMEM)
    return pl.pallas_call(
        output_kernel,
        in_specs=[whole] * 4,
        out_specs=whole,
        out_shape=jax.ShapeDtypeStruct((T, HEADS, D), bf16),
        scratch_shapes=[pltpu.VMEM((HEADS, T, D), f32)],
        compiler_params=pltpu.CompilerParams(vmem_limit_bytes=48 * 2**20),
    )(qo, m, gains, gate)


def local(queries, keys, values, betas, gate, gain):
    keys_h = jnp.transpose(keys, (1, 0, 2, 3)).reshape(HEADS, N, D)
    values_h = jnp.transpose(values, (1, 0, 2, 3)).reshape(HEADS, N, D)
    queries_h = jnp.transpose(queries, (1, 0, 2))
    betas_h = jnp.transpose(betas, (0, 2, 1)).reshape(N, HEADS).astype(f32)
    qo, m, gains = states(keys_h, values_h, queries_h, betas_h, jnp.pad(gain, ((0, 6), (0, 0))))
    return outputs(qo, m, gains, gate)


def solution(mesh):
    return jax.shard_map(
        local,
        mesh=mesh,
        in_specs=(
            P(("seq", "head"), None, None),
            P(("seq", "head"), None, None, None),
            P(("seq", "head"), None, None, None),
            P(("seq", "head"), None, None),
            P(("seq", "head"), None, None),
            P("head", None),
        ),
        out_specs=P(("seq", "head"), None, None),
        check_vma=False,
    )
```

time: 112 us -> 104 us (0.929)
  the two profiles are of different devices: /device:TPU:1 before, /device:TPU:25 now
where the time goes in v2:
time: 104 us
  Pallas kernels  98 us (94%)
  local copies, waits for them, and re-layouts  5.23 us (5%)
    pallas_call x1, Pallas kernels, states(): pl.pallas_call(states_kernel, in_specs=[whole] * 5, out_specs=[whole] * 3...  96 us
    transpose x1, local copies, waits for them, and re-layouts, local(): keys_h = jnp.transpose(keys, (1, 0, 2, 3)).reshape(HEADS, N, D)  2.19 us

profile of v2, /device:TPU:25, one launch (start us, length us, event | category | flops | bytes accessed | tf_op | source)
XLA Modules:
  0.0 104.0 jit_solution(11515881475130494503)
XLA Ops:
  0.0 0.0 copy-start.1
  0.0 0.8 pad.4.gain_ref
  0.8 0.7 convert_bitcast_fusion
  1.5 0.1 copy.10
  1.6 1.2 %copy.12 = bf16[128,16,128]{2,0,1:T(8,128)(2,1)S(1)} copy(bf16[128,16,128]{2,1,0:T(8,128)(2,1)} %param.6) | data formatting | bytes 1048576 | tf_op args[0]
  2.8 2.2 %copy.7 = bf16[16,128,2,128]{3,2,1,0:T(2,128)(2,1)S(1)} copy(bf16[16,128,2,128]{3,2,0,1:T(2,128)(2,1)} %bitcast.14) | data formatting | bytes 2097152 | tf_op jit(solution)/shard_map/transpose | solution.py:530
  5.0 0.0 copy-done.1
  5.0 0.0 copy-start
  5.0 1.0 copy.8
  6.0 96.0 %shard_map.64 = (f32[16,128,256]{2,1,0:T(8,128)S(1)}, f32[16,128,128]{2,1,0:T(8,128)S(1)}, f32[8,8,128]{2,1,0:T(8,128)S(1)}) custom-call(bf16[16,256,128]{2,1,0:T(8,128)(2,1)S(1)} %bitcast.10, bf16[16,256,128]{2,1,0:T(8,128)(2,1)S(1)} %bitcast.11, bf16[16,128,128]{2,1,0:T(8,128)(2,1)S(1)} %bitcast.12, f32[256,16]{1,0:T(8,128)S(1)} %bitcast.13, ...), custom_call_target="tpu_custom_call" | custom-call | tf_op jit(solution)/shard_map/pallas_call | solution.py:482
  102.0 0.0 copy-done
  102.0 2.0 %shard_map.65 = bf16[128,16,128]{2,1,0:T(8,128)(2,1)} custom-call(f32[16,128,256]{2,1,0:T(8,128)S(1)} %get-tuple-element.8.qo_ref, f32[16,128,128]{2,1,0:T(8,128)S(1)} %get-tuple-element.9.m_ref, f32[8,8,128]{2,1,0:T(8,128)S(1)} %get-tuple-element.10.gains_ref, bf16[128,16,128]{2,1,0:T(8,128)(2,1)S(1)} %copy-done), custom_call_target="tpu_custom_call" | custom-call | tf_op jit(solution)/shard_map/pallas_call | solution.py:519
Async XLA Ops:
  0.0 5.0 %copy-start.1 = (bf16[128,16,2,128]{3,2,1,0:T(2,128)(2,1)S(1)}, bf16[128,16,2,128]{3,2,1,0:T(2,128)(2,1)}, u32[]{:S(2)}) copy-start(bf16[128,16,2,128]{3,2,1,0:T(2,128)(2,1)} %param.8) | copy-start | bytes 3145732
  5.0 97.0 %copy-start = (bf16[128,16,128]{2,1,0:T(8,128)(2,1)S(1)}, bf16[128,16,128]{2,1,0:T(8,128)(2,1)}, u32[]{:S(2)}) copy-start(bf16[128,16,128]{2,1,0:T(8,128)(2,1)} %gate_ref.1) | copy-start | bytes 1572868

commit v3 on v2

v3 whole, which is shorter than its diff:
```python
import functools
import jax, jax.numpy as jnp
from jax import lax
from jax.experimental import pallas as pl
from jax.experimental.pallas import tpu as pltpu
from jax.sharding import PartitionSpec as P
f32, bf16 = jnp.float32, jnp.bfloat16
D = 128
N = 256
T = 128
BASE = 16

def split(a):
    hi = a.astype(bf16)
    return hi, (a - hi.astype(f32)).astype(bf16)

def mm(a, b):
    return lax.dot_general(a, b, (((1,), (0,)), ((), ())), preferred_element_type=f32)

def mm_nt(a, b):
    return lax.dot_general(a, b, (((1,), (1,)), ((), ())), preferred_element_type=f32)

def mm_tn(a, b):
    return lax.dot_general(a, b, (((0,), (0,)), ((), ())), preferred_element_type=f32)

def dot3(a, b):
    ah, al = split(a)
    bh, bl = split(b)
    return dot3s(ah, al, bh, bl)

def dot3s(ah, al, bh, bl):
    if ah.shape[1] == 128:
        return mm(jnp.concatenate([ah, al], 1), jnp.concatenate([bh, bh], 0)) + mm(ah, bl)
    return mm(ah, bh) + (mm(al, bh) + mm(ah, bl))

def unit_lower_inverses(lows):
    n = len(lows)
    lane = lax.broadcasted_iota(jnp.int32, (BASE, 128), 1)
    row = lax.broadcasted_iota(jnp.int32, (BASE, 128), 0)
    blk = lane // BASE
    packed = []
    for low in lows:
        z = jnp.zeros((BASE, 128), f32)
        for b in range(128 // BASE):
            z = jnp.where(blk == b, low[BASE * b:BASE * (b + 1), :], z)
        packed.append(jnp.where(row > lane % BASE, z, 0.0))
    eye = jnp.where(row == lane % BASE, 1.0, 0.0).astype(f32)
    xs = [eye for _ in lows]
    for j in range(BASE - 1):
        idx = blk * BASE + j
        for i in range(n):
            lj = jnp.take_along_axis(packed[i], idx, axis=1, mode="promise_in_bounds")
            xs[i] = xs[i] - lj * xs[i][j:j + 1, :]
    fulls = []
    for x in xs:
        fulls.append(jnp.concatenate([jnp.where(blk == b, x, 0.0) for b in range(128 // BASE)], axis=0))
    m = BASE
    r2 = lax.broadcasted_iota(jnp.int32, (128, 128), 0)
    c2 = lax.broadcasted_iota(jnp.int32, (128, 128), 1)
    while m < 128:
        offmask = ((r2 // m) % 2 == 1) & (c2 // m == r2 // m - 1)
        xos = [jnp.concatenate([x[m * (2 * b + 1):m * (2 * b + 2), :] for b in range(64 // m)], 0) for x in fulls]
        offs = [split(jnp.where(offmask, low, 0.0)) for low in lows]
        xos_s = [split(xo) for xo in xos]
        xs_s = [split(x) for x in fulls]
        ys = [dot3s(*xo, *off) for xo, off in zip(xos_s, offs)]
        ys = [split(y) for y in ys]
        zs = [xo - dot3s(*y, *x) for xo, y, x in zip(xos, ys, xs_s)]
        out = []
        for x, z in zip(fulls, zs):
            rows = []
            for b in range(64 // m):
                rows.append(x[m * 2 * b:m * (2 * b + 1), :])
                rows.append(z[m * b:m * (b + 1), :])
            out.append(jnp.concatenate(rows, 0))
        fulls = out
        m *= 2
    return fulls

MESH = pl.DeviceIdType.MESH
HEADS = 16
NX, NL, NG, NY = 4, 4, 4, 4
PAIR, ROW, LOW, HIGH, YS, LOW_BACK, ROW_BACK, BACK, GAIN, GAIN_ROW, SEMS = 0, 8, 16, 24, 32, 40, 48, 56, 64, 65, 69


def local_solves(keys, values, betas):
    hs = range(len(keys))
    r2 = lax.broadcasted_iota(jnp.int32, (128, 128), 0)
    c2 = lax.broadcasted_iota(jnp.int32, (128, 128), 1)
    eye = jnp.where(r2 == c2, 1.0, 0.0).astype(f32)
    lows, crosses, rights = [], [], []
    for k, v, beta in zip(keys, values, betas):
        kf = k.astype(f32)
        ssq = jnp.sum(kf * kf, axis=1, keepdims=True) + 1e-6
        p = beta / ssq
        bs = beta * lax.rsqrt(ssq)
        gram = mm_nt(k, k)
        lows.append(jnp.where(r2 > c2, p[:128] * gram[:128, :128], 0.0))
        lows.append(jnp.where(r2 > c2, p[128:] * gram[128:, 128:], 0.0))
        crosses.append(p[128:] * gram[128:, :128])
        rights.append(jnp.concatenate([p * kf, bs * v.astype(f32)], axis=1))
    invs = unit_lower_inverses(lows)
    y1 = [dot3(invs[2 * h], rights[h][:128]) for h in hs]
    rest = [rights[h][128:] - dot3(crosses[h], y1[h]) for h in hs]
    y2 = [dot3(invs[2 * h + 1], rest[h]) for h in hs]
    ys = [split(jnp.concatenate([y1[h], y2[h]], 0)) for h in hs]
    kys = [mm_tn(keys[h], ys[h][0]) + mm_tn(keys[h], ys[h][1]) for h in hs]
    return ys, [(eye - ky[:, :D], ky[:, D:]) for ky in kys]


def local_outputs(queries, keys, ys):
    vis = lax.broadcasted_iota(jnp.int32, (T, N), 1) <= 2 * lax.broadcasted_iota(jnp.int32, (T, N), 0) + 1
    scores = [split(jnp.where(vis, mm_nt(q, k), 0.0)) for q, k in zip(queries, keys)]
    sys_ = [dot3s(*s, *y) for s, y in zip(scores, ys)]
    return [(q.astype(f32) - sy[:, :D], sy[:, D:]) for q, sy in zip(queries, sys_)]


def compose(late, early):
    joined = dot3(late[:, :D], early)
    return jnp.concatenate([joined[:, :D], joined[:, D:] + late[:, D:]], axis=1)


def advance(pair, state):
    return dot3(pair[:, :D], state) + pair[:, D:]


def states_kernel(
    k_ref, v_ref, q_ref, b_ref, gain_ref, qo_ref, m_ref, gains_ref,
    pool, chip, row_in, row_pre, row_tot, low_in, low_pre, low_tot,
    high_in, high_pre, high_tot, y_in, start, low_out, low_state,
    row_out, chip_state, after, send, recv,
):
    seq, head = lax.axis_index("seq"), lax.axis_index("head")
    x, c = head // 2, head % 2
    y, g, l = seq // (NG * NL), (seq // NL) % NG, seq % NL
    oc = 1 - c

    def meet(gg):
        return 2 - c + (((gg + 1) // 2) % 2) * (2 * c - 1)

    hub = meet(g)
    is_hub = l == hub

    def device(xx=None, cc=None, yy=None, gg=None, ll=None):
        xx, cc = x if xx is None else xx, c if cc is None else cc
        yy, gg, ll = y if yy is None else yy, g if gg is None else gg, l if ll is None else ll
        return {"seq": (yy * NG + gg) * NL + ll, "head": xx * 2 + cc}

    partner = device(cc=oc)

    def remote(src, dst, s, r, where):
        return pltpu.make_async_remote_copy(
            src_ref=src, dst_ref=dst, send_sem=send.at[s], recv_sem=recv.at[r],
            device_id=where, device_id_type=MESH,
        )

    barrier = pltpu.get_barrier_semaphore()

    def greet(peers):
        for peer in peers:
            pl.semaphore_signal(barrier, inc=1, device_id=peer, device_id_type=MESH)

    greet([partner] + [device(xx=(x + k) % NX) for k in (1, 2, 3)])

    @pl.when(is_hub)
    def _():
        greet([device(ll=(l + k) % NL) for k in (1, 2, 3)])
        greet([device(gg=(g + k) % NG, ll=meet((g + k) % NG)) for k in (1, 2, 3)])
        greet([device(yy=(y + k) % NY) for k in (1, 2, 3)])

    @pl.when(l != hub)
    def _():
        greet([device(ll=hub)])

    gains_ref[head] = gain_ref[...]

    @pl.when(is_hub)
    def _():
        pl.semaphore_wait(barrier, 13)

    @pl.when(l != hub)
    def _():
        pl.semaphore_wait(barrier, 5)

    def gain_copy():
        return remote(gain_ref, gains_ref.at[head], GAIN, GAIN, partner)

    def gain_row_copy(k, there, origin):
        rows = gains_ref.at[pl.ds(2 * origin, 2)]
        return remote(rows, rows, GAIN_ROW + k, GAIN_ROW + origin, device(xx=there))

    def pair_copy(i):
        return remote(pool.at[oc, i], pool.at[2, i], PAIR + i, PAIR + i, partner)

    def row_copy(e, k, there, origin):
        return remote(
            chip.at[2 * there + e], row_in.at[e, origin], ROW + 4 * e + k, ROW + 4 * e + origin, device(xx=there)
        )

    def low_copy(e, there, origin):
        return remote(row_tot.at[e], low_in.at[e, origin], LOW + 4 * e, LOW + 4 * e + origin, device(ll=there))

    def high_copy(e, k, there, origin):
        return remote(
            low_tot.at[e], high_in.at[e, origin], HIGH + 4 * e + k, HIGH + 4 * e + origin,
            device(gg=there, ll=meet(there)),
        )

    def y_copy(e, k, there, origin):
        return remote(high_tot.at[e], y_in.at[e, origin], YS + 4 * e + k, YS + 4 * e + origin, device(yy=there))

    def low_back(e, there):
        return remote(
            low_out.at[e, there], low_state.at[e], LOW_BACK + 4 * e + there, LOW_BACK + 4 * e, device(ll=there)
        )

    def row_back(e, k, there, origin):
        return remote(
            row_out.at[e, there], chip_state.at[2 * origin + e], ROW_BACK + 4 * e + k, ROW_BACK + 4 * e + origin,
            device(xx=there),
        )

    def back_copy(src, i):
        return remote(src.at[i], m_ref.at[8 * c + i], BACK + i, BACK + i, partner)

    def joint(parts, e, pre, tot):
        first = compose(parts[e, 1], parts[e, 0])
        last = compose(parts[e, 3], parts[e, 2])
        tot[e] = compose(last, first)
        pre[e, 0] = parts[e, 0]
        pre[e, 1] = first

    def third(parts, e, pre):
        pre[e, 2] = compose(parts[e, 2], pre[e, 1])

    def join_chip(e):
        for k in (2, 1, 3, 0):
            there = (x + k) % NX
            i = 2 * there + e
            pair_copy(i).wait_recv()
            joined = compose(pool[2 - c, i], pool[2 * c, i])
            if k:
                chip[i] = joined
                row_copy(e, k, there, x).start()
            else:
                row_in[e, x] = joined

    def up_row(e):
        for k in (1, 2, 3):
            origin = (x + k) % NX
            row_copy(e, 0, origin, origin).wait_recv()
        joint(row_in, e, row_pre, row_tot)

        @pl.when(l != hub)
        def _():
            low_copy(e, hub, l).start()

        @pl.when(is_hub)
        def _():
            low_in[e, l] = row_tot[e]

        third(row_in, e, row_pre)

    def up_low(e):
        @pl.when(is_hub)
        def _():
            for k in (1, 2, 3):
                origin = (l + k) % NL
                low_copy(e, origin, origin).wait_recv()
            joint(low_in, e, low_pre, low_tot)
            for k in (2, 1, 3):
                high_copy(e, k, (g + k) % NG, g).start()
            high_in[e, g] = low_tot[e]
            third(low_in, e, low_pre)

    def up_high(e):
        @pl.when(is_hub)
        def _():
            for k in (1, 2, 3):
                origin = (g + k) % NG
                high_copy(e, k, origin, origin).wait_recv()
            joint(high_in, e, high_pre, high_tot)
            for k in (2, 1, 3):
                @pl.when(y + k < NY)
                def _():
                    y_copy(e, k, (y + k) % NY, y).start()
            third(high_in, e, high_pre)

    def down_high(e):
        @pl.when(is_hub)
        def _():
            start[e] = jnp.zeros((D, D), f32)
            for s in (0, 1, 2):
                @pl.when(y > s)
                def _():
                    y_copy(e, 0, s, s).wait_recv()
                    start[e] = advance(y_in[e, s], start[e])

            @pl.when(g > 0)
            def _():
                start[e] = advance(high_pre[e, g - 1], start[e])

            begin = start[e]
            for place in range(NL):
                low_out[e, place] = begin if place == 0 else advance(low_pre[e, place - 1], begin)

                @pl.when(l != place)
                def _():
                    low_back(e, place).start()

                @pl.when(l == place)
                def _():
                    low_state[e] = low_out[e, place]

    def down_row(e):
        @pl.when(l != hub)
        def _():
            low_back(e, hub).wait_recv()
        begin = low_state[e]
        for place in range(NX):
            row_out[e, place] = begin if place == 0 else advance(row_pre[e, place - 1], begin)
        for k in (2, 1, 3):
            row_back(e, k, (x + k) % NX, x).start()
        chip_state[2 * x + e] = row_out[e, x]

    def down_chip(e):
        for k in (0, 1, 3, 2):
            origin = (x + k) % NX
            i = 2 * origin + e
            if k:
                row_back(e, 0, origin, origin).wait_recv()

            @pl.when(c == 1)
            def _():
                back_copy(chip_state, i).start()

            begin = chip_state[i]
            end = advance(pool[2 * c, i], begin)

            @pl.when(c == 0)
            def _():
                after[i] = end
                back_copy(after, i).start()
                m_ref[i] = begin

            @pl.when(c == 1)
            def _():
                m_ref[8 + i] = end

    gain_copy().start()
    lane = lax.broadcasted_iota(jnp.int32, (N, HEADS), 1)

    def turn(t, carry):
        e, half = t // 2, t % 2
        here = [2 * v + e for v in range(NX)]
        betas = [
            jnp.sum(jnp.where(lane == 8 * half + i, b_ref[...], 0.0), axis=1, keepdims=True) for i in here
        ]
        keys = [k_ref[8 * half + i] for i in here]
        ys, maps = local_solves(keys, [v_ref[8 * half + i] for i in here], betas)
        for i, (a_part, b_part) in zip(here, maps):
            pool[half, i, :, :D] = a_part
            pool[half, i, :, D:] = b_part

        @pl.when(half != c)
        def _():
            for i in here:
                pair_copy(i).start()

        outs = local_outputs([q_ref[8 * half + i] for i in here], keys, ys)
        for i, (q_part, o_part) in zip(here, outs):
            qo_ref[8 * half + i, :, :D] = q_part
            qo_ref[8 * half + i, :, D:] = o_part

        @pl.when(t == 1 + c)
        def _():
            join_chip(0)

        @pl.when((t == 2) & (c == 0))
        def _():
            up_row(0)

        return carry

    lax.fori_loop(0, 4, turn, 0)

    def on_core(which, step):
        @pl.when(c == which)
        def _():
            step()

    on_core(1, lambda: up_row(0))
    join_chip(1)
    remote(gain_ref, gains_ref.at[2 * x + oc], GAIN, GAIN, partner).wait_recv()
    for k in (1, 2, 3):
        gain_row_copy(k, (x + k) % NX, x).start()
    on_core(0, lambda: up_low(0))
    up_row(1)
    on_core(1, lambda: up_low(0))
    on_core(0, lambda: up_high(0))
    up_low(1)
    on_core(1, lambda: up_high(0))
    down_high(0)
    up_high(1)
    down_row(0)
    on_core(0, lambda: down_chip(0))
    down_high(1)
    on_core(1, lambda: down_chip(0))
    down_row(1)
    down_chip(1)
    for i in range(8):
        remote(after.at[i], m_ref.at[8 * oc + i], BACK + i, BACK + i, partner).wait_recv()
    for k in (1, 2, 3):
        origin = (x + k) % NX
        gain_row_copy(k, origin, origin).wait_recv()

    gain_copy().wait_send()
    for k in (1, 2, 3):
        gain_row_copy(k, (x + k) % NX, x).wait_send()
    for i in range(8):
        pair_copy(i).wait_send()
        back_copy(after, i).wait_send()
    for e in range(2):
        for k in (1, 2, 3):
            row_copy(e, k, (x + k) % NX, x).wait_send()
            row_back(e, k, (x + k) % NX, x).wait_send()

        @pl.when(l != hub)
        def _():
            low_copy(e, hub, l).wait_send()

        @pl.when(is_hub)
        def _():
            for place in range(NL):
                @pl.when(l != place)
                def _():
                    low_back(e, place).wait_send()
            for k in (1, 2, 3):
                high_copy(e, k, (g + k) % NG, g).wait_send()

                @pl.when(y + k < NY)
                def _():
                    y_copy(e, k, (y + k) % NY, y).wait_send()


def states(keys, values, queries, betas, gain):
    wide, square = (D, 2 * D), (D, D)
    whole = pl.BlockSpec(memory_space=pltpu.VMEM)

    def vm(*shape):
        return pltpu.VMEM(shape, f32)

    return pl.pallas_call(
        states_kernel,
        in_specs=[whole] * 5,
        out_specs=[whole] * 3,
        out_shape=[
            jax.ShapeDtypeStruct((HEADS, T, 2 * D), f32),
            jax.ShapeDtypeStruct((HEADS, D, D), f32),
            jax.ShapeDtypeStruct((8, 8, D), f32),
        ],
        scratch_shapes=[
            vm(3, 8, *wide), vm(8, *wide),
            vm(2, NX, *wide), vm(2, 3, *wide), vm(2, *wide),
            vm(2, NL, *wide), vm(2, 3, *wide), vm(2, *wide),
            vm(2, NG, *wide), vm(2, 3, *wide), vm(2, *wide),
            vm(2, NY, *wide), vm(2, *square), vm(2, NL, *square), vm(2, *square),
            vm(2, NX, *square), vm(8, *square), vm(8, *square),
            pltpu.SemaphoreType.DMA((SEMS,)), pltpu.SemaphoreType.DMA((SEMS,)),
        ],
        compiler_params=pltpu.CompilerParams(
            collective_id=0, has_side_effects=True, vmem_limit_bytes=48 * 2**20
        ),
    )(keys, values, queries, betas, gain)


def output_kernel(qo_ref, m_ref, gains_ref, gate_ref, out_ref, rows):
    for h in range(HEADS):
        r = dot3(qo_ref[h, :, :D], m_ref[h]) + qo_ref[h, :, D:]
        scale = lax.rsqrt(jnp.mean(r * r, axis=-1, keepdims=True) + 1e-6)
        rows[h] = r * scale * gains_ref[h // 2, h % 2 : h % 2 + 1, :]
    gate = gate_ref[...].astype(f32)
    normed = jnp.swapaxes(rows[...], 0, 1)
    out_ref[...] = (normed * (gate / (1.0 + jnp.exp(-gate)))).astype(bf16)


def outputs(qo, m, gains, gate):
    whole = pl.BlockSpec(memory_space=pltpu.VMEM)
    return pl.pallas_call(
        output_kernel,
        in_specs=[whole] * 4,
        out_specs=whole,
        out_shape=jax.ShapeDtypeStruct((T, HEADS, D), bf16),
        scratch_shapes=[pltpu.VMEM((HEADS, T, D), f32)],
        compiler_params=pltpu.CompilerParams(vmem_limit_bytes=48 * 2**20),
    )(qo, m, gains, gate)


def local(queries, keys, values, betas, gate, gain):
    keys_h = jnp.transpose(keys, (1, 0, 2, 3)).reshape(HEADS, N, D)
    values_h = jnp.transpose(values, (1, 0, 2, 3)).reshape(HEADS, N, D)
    queries_h = jnp.transpose(queries, (1, 0, 2))
    betas_h = jnp.transpose(betas, (0, 2, 1)).reshape(N, HEADS).astype(f32)
    qo, m, gains = states(keys_h, values_h, queries_h, betas_h, jnp.pad(gain, ((0, 6), (0, 0))))
    return outputs(qo, m, gains, gate)


def solution(mesh):
    return jax.shard_map(
        local,
        mesh=mesh,
        in_specs=(
            P(("seq", "head"), None, None),
            P(("seq", "head"), None, None, None),
            P(("seq", "head"), None, None, None),
            P(("seq", "head"), None, None),
            P(("seq", "head"), None, None),
            P("head", None),
        ),
        out_specs=P(("seq", "head"), None, None),
        check_vma=False,
    )
```

time: 104 us -> 87.7 us (0.84); the launches traced: 104 us -> 86.1 us
  Pallas kernels: 98 us -> 80.1 us
    pallas_call x1, Pallas kernels: 96 us -> 78.1 us  [states(): pl.pallas_call(states_kernel, in_specs=[whole] * 5, out_specs=[whole] * 3...]
where the time goes in v3:
time: 87.7 us; the launch traced here: 86.1 us
  Pallas kernels  80.1 us (91%)
  local copies, waits for them, and re-layouts  5.23 us (6%)
    pallas_call x1, Pallas kernels, states(): pl.pallas_call(states_kernel, in_specs=[whole] * 5, out_specs=[whole] * 3...  78.1 us
    transpose x1, local copies, waits for them, and re-layouts, local(): keys_h = jnp.transpose(keys, (1, 0, 2, 3)).reshape(HEADS, N, D)  2.19 us
    pallas_call x1, Pallas kernels, outputs(): pl.pallas_call(output_kernel, in_specs=[whole] * 4, out_specs=whole, out_...  2.02 us

profile of v3, /device:TPU:25, one launch (start us, length us, event | category | flops | bytes accessed | tf_op | source)
XLA Modules:
  0.0 86.1 jit_solution(1154619518680750006)
XLA Ops:
  0.0 0.0 copy-start.1
  0.0 0.8 pad.4.gain_ref
  0.8 0.7 convert_bitcast_fusion
  1.5 0.1 copy.10
  1.6 1.2 %copy.12 = bf16[128,16,128]{2,0,1:T(8,128)(2,1)S(1)} copy(bf16[128,16,128]{2,1,0:T(8,128)(2,1)} %param.6) | data formatting | bytes 1048576 | tf_op args[0]
  2.8 2.2 %copy.7 = bf16[16,128,2,128]{3,2,1,0:T(2,128)(2,1)S(1)} copy(bf16[16,128,2,128]{3,2,0,1:T(2,128)(2,1)} %bitcast.14) | data formatting | bytes 2097152 | tf_op jit(solution)/shard_map/transpose | solution.py:500
  5.0 0.0 copy-done.1
  5.0 0.0 copy-start
  5.0 1.0 %copy.8 = bf16[16,128,2,128]{3,2,1,0:T(2,128)(2,1)S(1)} copy(bf16[16,128,2,128]{3,2,0,1:T(2,128)(2,1)S(1)} %bitcast.15) | data formatting | bytes 2097152 | tf_op jit(solution)/shard_map/transpose | solution.py:501
  6.0 78.1 %shard_map.64 = (f32[16,128,256]{2,1,0:T(8,128)S(1)}, f32[16,128,128]{2,1,0:T(8,128)S(1)}, f32[8,8,128]{2,1,0:T(8,128)S(1)}) custom-call(bf16[16,256,128]{2,1,0:T(8,128)(2,1)S(1)} %bitcast.10, bf16[16,256,128]{2,1,0:T(8,128)(2,1)S(1)} %bitcast.11, bf16[16,128,128]{2,1,0:T(8,128)(2,1)S(1)} %bitcast.12, f32[256,16]{1,0:T(8,128)S(1)} %bitcast.13, ...), custom_call_target="tpu_custom_call" | custom-call | tf_op jit(solution)/shard_map/pallas_call | solution.py:453
  84.1 0.0 copy-done
  84.1 2.0 %shard_map.65 = bf16[128,16,128]{2,1,0:T(8,128)(2,1)} custom-call(f32[16,128,256]{2,1,0:T(8,128)S(1)} %get-tuple-element.8.qo_ref, f32[16,128,128]{2,1,0:T(8,128)S(1)} %get-tuple-element.9.m_ref, f32[8,8,128]{2,1,0:T(8,128)S(1)} %get-tuple-element.10.gains_ref, bf16[128,16,128]{2,1,0:T(8,128)(2,1)S(1)} %copy-done), custom_call_target="tpu_custom_call" | custom-call | tf_op jit(solution)/shard_map/pallas_call | solution.py:489
Async XLA Ops:
  0.0 5.0 %copy-start.1 = (bf16[128,16,2,128]{3,2,1,0:T(2,128)(2,1)S(1)}, bf16[128,16,2,128]{3,2,1,0:T(2,128)(2,1)}, u32[]{:S(2)}) copy-start(bf16[128,16,2,128]{3,2,1,0:T(2,128)(2,1)} %param.8) | copy-start | bytes 3145732
  5.0 79.1 %copy-start = (bf16[128,16,128]{2,1,0:T(8,128)(2,1)S(1)}, bf16[128,16,128]{2,1,0:T(8,128)(2,1)}, u32[]{:S(2)}) copy-start(bf16[128,16,128]{2,1,0:T(8,128)(2,1)} %gate_ref.1) | copy-start | bytes 1572868

commit v4 on v3

--- a/solution.py
+++ b/solution.py
@@ -128,7 +128,7 @@
     k_ref, v_ref, q_ref, b_ref, gain_ref, qo_ref, m_ref, gains_ref,
     pool, chip, row_in, row_pre, row_tot, low_in, low_pre, low_tot,
     high_in, high_pre, high_tot, y_in, start, low_out, low_state,
-    row_out, chip_state, after, send, recv,
+    row_out, chip_state, after, send, recv, near,
 ):
     seq, head = lax.axis_index("seq"), lax.axis_index("head")
     x, c = head // 2, head % 2
@@ -155,32 +155,43 @@
         )
 
     barrier = pltpu.get_barrier_semaphore()
+    rows = [device(xx=(x + k) % NX) for k in (1, 2, 3)]
 
     def greet(peers):
         for peer in peers:
             pl.semaphore_signal(barrier, inc=1, device_id=peer, device_id_type=MESH)
 
-    greet([partner] + [device(xx=(x + k) % NX) for k in (1, 2, 3)])
-
     @pl.when(is_hub)
     def _():
         greet([device(ll=(l + k) % NL) for k in (1, 2, 3)])
+        greet([device(xx=(x + k) % NX, cc=oc) for k in (0, 1, 2, 3)])
         greet([device(gg=(g + k) % NG, ll=meet((g + k) % NG)) for k in (1, 2, 3)])
-        greet([device(yy=(y + k) % NY) for k in (1, 2, 3)])
+        for k in (1, 2, 3):
+            @pl.when(y >= k)
+            def _():
+                greet([device(yy=(y + NY - k) % NY)])
 
     @pl.when(l != hub)
     def _():
-        greet([device(ll=hub)])
+        greet(rows)
+
+    @pl.when((l != hub) & (l != 3 - hub))
+    def _():
+        greet([partner])
+
+    def near_met():
+        @pl.when((l != hub) & (l != 3 - hub))
+        def _():
+            pl.semaphore_wait(barrier, 5)
+            pl.semaphore_signal(near, inc=1, device_id=device(ll=hub), device_id_type=MESH)
+
+        @pl.when(l == 3 - hub)
+        def _():
+            pl.semaphore_wait(barrier, 8)
+            pl.semaphore_signal(near, inc=1, device_id=device(ll=hub), device_id_type=MESH)
+            pl.semaphore_signal(near, inc=1, device_id=partner, device_id_type=MESH)
 
     gains_ref[head] = gain_ref[...]
-
-    @pl.when(is_hub)
-    def _():
-        pl.semaphore_wait(barrier, 13)
-
-    @pl.when(l != hub)
-    def _():
-        pl.semaphore_wait(barrier, 5)
 
     def gain_copy():
         return remote(gain_ref, gains_ref.at[head], GAIN, GAIN, partner)
@@ -268,6 +279,8 @@
                 origin = (l + k) % NL
                 low_copy(e, origin, origin).wait_recv()
             joint(low_in, e, low_pre, low_tot)
+            if e == 0:
+                pl.semaphore_wait(barrier, 6 - y)
             for k in (2, 1, 3):
                 high_copy(e, k, (g + k) % NG, g).start()
             high_in[e, g] = low_tot[e]
@@ -347,7 +360,6 @@
             def _():
                 m_ref[8 + i] = end
 
-    gain_copy().start()
     lane = lax.broadcasted_iota(jnp.int32, (N, HEADS), 1)
 
     def turn(t, carry):
@@ -362,10 +374,27 @@
             pool[half, i, :, :D] = a_part
             pool[half, i, :, D:] = b_part
 
-        @pl.when(half != c)
+        @pl.when(t == 0)
+        def _():
+            near_met()
+
+        @pl.when((t == 1) & is_hub)
+        def _():
+            pl.semaphore_wait(near, 4)
+
+        @pl.when((t == 1) & is_hub & (c == 1))
+        def _():
+            for v in range(NX):
+                pair_copy(2 * v).start()
+
+        @pl.when((half != c) & ((t > 0) | (l != hub)))
         def _():
             for i in here:
                 pair_copy(i).start()
+
+        @pl.when(t == 1)
+        def _():
+            gain_copy().start()
 
         outs = local_outputs([q_ref[8 * half + i] for i in here], keys, ys)
         for i, (q_part, o_part) in zip(here, outs):
@@ -457,7 +486,7 @@
         out_shape=[
             jax.ShapeDtypeStruct((HEADS, T, 2 * D), f32),
             jax.ShapeDtypeStruct((HEADS, D, D), f32),
-            jax.ShapeDtypeStruct((8, 8, D), f32),
+            jax.ShapeDtypeStruct((8, 2, D), f32),
         ],
         scratch_shapes=[
             vm(3, 8, *wide), vm(8, *wide),
@@ -466,12 +495,44 @@
             vm(2, NG, *wide), vm(2, 3, *wide), vm(2, *wide),
             vm(2, NY, *wide), vm(2, *square), vm(2, NL, *square), vm(2, *square),
             vm(2, NX, *square), vm(8, *square), vm(8, *square),
-            pltpu.SemaphoreType.DMA((SEMS,)), pltpu.SemaphoreType.DMA((SEMS,)),
+            pltpu.SemaphoreType.DMA((SEMS,)), pltpu.SemaphoreType.DMA((SEMS,)), pltpu.SemaphoreType.REGULAR,
         ],
         compiler_params=pltpu.CompilerParams(
             collective_id=0, has_side_effects=True, vmem_limit_bytes=48 * 2**20
         ),
     )(keys, values, queries, betas, gain)
+
+
+def by_head_kernel(k_ref, v_ref, q_ref, ko_ref, vo_ref, qo_ref, held, sem, q_sem):
+    fetch = pltpu.make_async_copy(q_ref, held, q_sem)
+    fetch.start()
+    copies = [
+        pltpu.make_async_copy(src.at[:, h], dst.at[h], sem.at[n, h])
+        for h in range(HEADS)
+        for n, (src, dst) in enumerate(((k_ref, ko_ref), (v_ref, vo_ref)))
+    ]
+    for copy in copies:
+        copy.start()
+    fetch.wait()
+    qo_ref[...] = jnp.swapaxes(held[...].astype(f32), 0, 1).astype(bf16)
+    for copy in copies:
+        copy.wait()
+
+
+def by_head(keys, values, queries):
+    whole, away = pl.BlockSpec(memory_space=pltpu.VMEM), pl.BlockSpec(memory_space=pl.ANY)
+    pairs = jax.ShapeDtypeStruct((HEADS, T, 2, D), bf16)
+    k, v, q = pl.pallas_call(
+        by_head_kernel,
+        in_specs=[away] * 3,
+        out_specs=[whole] * 3,
+        out_shape=[pairs, pairs, jax.ShapeDtypeStruct((HEADS, T, D), bf16)],
+        scratch_shapes=[
+            pltpu.VMEM((T, HEADS, D), bf16), pltpu.SemaphoreType.DMA((2, HEADS)), pltpu.SemaphoreType.DMA,
+        ],
+        compiler_params=pltpu.CompilerParams(vmem_limit_bytes=50 * 2**20),
+    )(keys, values, queries)
+    return k.reshape(HEADS, N, D), v.reshape(HEADS, N, D), q
 
 
 def output_kernel(qo_ref, m_ref, gains_ref, gate_ref, out_ref, rows):
@@ -497,11 +558,9 @@
 
 
 def local(queries, keys, values, betas, gate, gain):
-    keys_h = jnp.transpose(keys, (1, 0, 2, 3)).reshape(HEADS, N, D)
-    values_h = jnp.transpose(values, (1, 0, 2, 3)).reshape(HEADS, N, D)
-    queries_h = jnp.transpose(queries, (1, 0, 2))
+    keys_h, values_h, queries_h = by_head(keys, values, queries)
     betas_h = jnp.transpose(betas, (0, 2, 1)).reshape(N, HEADS).astype(f32)
-    qo, m, gains = states(keys_h, values_h, queries_h, betas_h, jnp.pad(gain, ((0, 6), (0, 0))))
+    qo, m, gains = states(keys_h, values_h, queries_h, betas_h, gain)
     return outputs(qo, m, gains, gate)
 
 

time: 87.7 us -> 83.8 us (0.956)
  local copies, waits for them, and re-layouts: 5.23 us -> 1.17 us
    transpose x2 -> x0, local copies, waits for them, and re-layouts: 3.15 us -> none  [the longest x1 2.19 us: local(): keys_h = jnp.transpose(keys, (1, 0, 2, 3)).reshape(HEADS, N, D)]
    pallas_call x0 -> x1, Pallas kernels: none -> 2.18 us  [by_head(): pl.pallas_call(by_head_kernel, in_specs=[away] * 3, out_specs=[whole] * 3...]
    pallas_call x1, Pallas kernels: 78.1 us -> 76.6 us  [states(): pl.pallas_call(states_kernel, in_specs=[whole] * 5, out_specs=[whole] * 3...]
where the time goes in v4:
time: 83.8 us; the launch traced here: 82.8 us
  Pallas kernels  80.8 us (96%)
  local copies, waits for them, and re-layouts  1.17 us (1%)
    pallas_call x1, Pallas kernels, states(): pl.pallas_call(states_kernel, in_specs=[whole] * 5, out_specs=[whole] * 3...  76.6 us
    pallas_call x1, Pallas kernels, by_head(): pl.pallas_call(by_head_kernel, in_specs=[away] * 3, out_specs=[whole] * 3...  2.18 us
    pallas_call x1, Pallas kernels, outputs(): pl.pallas_call(output_kernel, in_specs=[whole] * 4, out_specs=whole, out_...  2.05 us

profile of v4, /device:TPU:25, one launch (start us, length us, event | category | flops | bytes accessed | tf_op | source)
XLA Modules:
  0.0 82.8 jit_solution(4844445870571128221)
XLA Ops:
  0.0 0.0 copy-start.2
  0.0 0.7 convert_bitcast_fusion
  0.7 0.1 copy.7
  0.8 0.0 copy-start
  0.9 1.0 %copy-done = bf16[128,16,128]{2,1,0:T(8,128)(2,1)S(1)} copy-done((bf16[128,16,128]{2,1,0:T(8,128)(2,1)S(1)}, bf16[128,16,128]{2,1,0:T(8,128)(2,1)}, u32[]{:S(2)}) %copy-start) | copy-done | bytes 524312
  1.9 0.0 copy-start.1
  1.9 2.2 %shard_map.64 = (bf16[16,128,2,128]{3,2,1,0:T(2,128)(2,1)S(1)}, bf16[16,128,2,128]{3,2,1,0:T(2,128)(2,1)S(1)}, bf16[16,128,128]{2,1,0:T(8,128)(2,1)S(1)}) custom-call(bf16[128,16,2,128]{3,2,1,0:T(2,128)(2,1)} %k_ref.1, bf16[128,16,2,128]{3,2,1,0:T(2,128)(2,1)} %v_ref.1, bf16[128,16,128]{2,1,0:T(8,128)(2,1)S(1)} %copy-done), custom_call_target="tpu_custom_call" | custom-call | tf_op jit(solution)/shard_map/pallas_call | solution.py:525
  4.1 0.0 copy-done.2
  4.1 76.6 %shard_map.65 = (f32[16,128,256]{2,1,0:T(8,128)S(1)}, f32[16,128,128]{2,1,0:T(8,128)S(1)}, f32[8,2,128]{2,1,0:T(2,128)S(1)}) custom-call(bf16[16,256,128]{2,1,0:T(8,128)(2,1)S(1)} %bitcast.5, bf16[16,256,128]{2,1,0:T(8,128)(2,1)S(1)} %bitcast.6, bf16[16,128,128]{2,1,0:T(8,128)(2,1)S(1)} %get-tuple-element.13.q_ref, f32[256,16]{1,0:T(8,128)S(1)} %bitcast.7, ...), custom_call_target="tpu_custom_call" | custom-call | tf_op jit(solution)/shard_map/pallas_call | solution.py:482
  80.7 0.0 copy-done.1
  80.7 2.0 %shard_map.66 = bf16[128,16,128]{2,1,0:T(8,128)(2,1)} custom-call(f32[16,128,256]{2,1,0:T(8,128)S(1)} %get-tuple-element.14.qo_ref, f32[16,128,128]{2,1,0:T(8,128)S(1)} %get-tuple-element.15.m_ref, f32[8,2,128]{2,1,0:T(2,128)S(1)} %get-tuple-element.16.gains_ref, bf16[128,16,128]{2,1,0:T(8,128)(2,1)S(1)} %copy-done.1), custom_call_target="tpu_custom_call" | custom-call | tf_op jit(solution)/shard_map/pallas_call | solution.py:550
Async XLA Ops:
  0.0 4.1 %copy-start.2 = (f32[2,128]{1,0:T(2,128)S(1)}, f32[2,128]{1,0:T(2,128)}, u32[]{:S(2)}) copy-start(f32[2,128]{1,0:T(2,128)} %gain_ref.1) | copy-start | bytes 3076
  0.8 1.0 %copy-start = (bf16[128,16,128]{2,1,0:T(8,128)(2,1)S(1)}, bf16[128,16,128]{2,1,0:T(8,128)(2,1)}, u32[]{:S(2)}) copy-start(bf16[128,16,128]{2,1,0:T(8,128)(2,1)} %q_ref.1) | copy-start | bytes 1572868
  1.9 78.8 %copy-start.1 = (bf16[128,16,128]{2,1,0:T(8,128)(2,1)S(1)}, bf16[128,16,128]{2,1,0:T(8,128)(2,1)}, u32[]{:S(2)}) copy-start(bf16[128,16,128]{2,1,0:T(8,128)(2,1)} %gate_ref.1) | copy-start | bytes 1572868

commit v5 on v4

--- a/solution.py
+++ b/solution.py
@@ -38,19 +38,27 @@
     lane = lax.broadcasted_iota(jnp.int32, (BASE, 128), 1)
     row = lax.broadcasted_iota(jnp.int32, (BASE, 128), 0)
     blk = lane // BASE
-    packed = []
+    half = BASE // 2
+    upper, lower = [], []
     for low in lows:
         z = jnp.zeros((BASE, 128), f32)
         for b in range(128 // BASE):
             z = jnp.where(blk == b, low[BASE * b:BASE * (b + 1), :], z)
-        packed.append(jnp.where(row > lane % BASE, z, 0.0))
+        z = jnp.where(row > lane % BASE, z, 0.0)
+        upper.append(z[:half])
+        lower.append(z[half:])
     eye = jnp.where(row == lane % BASE, 1.0, 0.0).astype(f32)
-    xs = [eye for _ in lows]
+    tops, ends = [eye[:half] for _ in lows], [eye[half:] for _ in lows]
+    blk = blk[:half]
     for j in range(BASE - 1):
         idx = blk * BASE + j
         for i in range(n):
-            lj = jnp.take_along_axis(packed[i], idx, axis=1, mode="promise_in_bounds")
-            xs[i] = xs[i] - lj * xs[i][j:j + 1, :]
+            pivot = tops[i][j:j + 1, :] if j < half else ends[i][j - half:j - half + 1, :]
+            ends[i] = ends[i] - jnp.take_along_axis(lower[i], idx, axis=1, mode="promise_in_bounds") * pivot
+            if j < half - 1:
+                tops[i] = tops[i] - jnp.take_along_axis(upper[i], idx, axis=1, mode="promise_in_bounds") * pivot
+    xs = [jnp.concatenate([top, end], 0) for top, end in zip(tops, ends)]
+    blk = lane // BASE
     fulls = []
     for x in xs:
         fulls.append(jnp.concatenate([jnp.where(blk == b, x, 0.0) for b in range(128 // BASE)], axis=0))
@@ -127,8 +135,8 @@
 def states_kernel(
     k_ref, v_ref, q_ref, b_ref, gain_ref, qo_ref, m_ref, gains_ref,
     pool, chip, row_in, row_pre, row_tot, low_in, low_pre, low_tot,
-    high_in, high_pre, high_tot, y_in, start, low_out, low_state,
-    row_out, chip_state, after, send, recv, near,
+    high_in, high_tot, y_in, start, low_out, low_state,
+    row_out, chip_state, after, y_high, y_low, send, recv, near,
 ):
     seq, head = lax.axis_index("seq"), lax.axis_index("head")
     x, c = head // 2, head % 2
@@ -219,6 +227,12 @@
 
     def y_copy(e, k, there, origin):
         return remote(high_tot.at[e], y_in.at[e, origin], YS + 4 * e + k, YS + 4 * e + origin, device(yy=there))
+
+    def y_copy_first(e, k, there):
+        part = pl.ds(D, D)
+        return remote(
+            high_tot.at[e, :, part], y_in.at[e, 0, :, part], YS + 4 * e + k, YS + 4 * e, device(yy=there)
+        )
 
     def low_back(e, there):
         return remote(
@@ -281,29 +295,34 @@
             joint(low_in, e, low_pre, low_tot)
             if e == 0:
                 pl.semaphore_wait(barrier, 6 - y)
-            for k in (2, 1, 3):
-                high_copy(e, k, (g + k) % NG, g).start()
+            for later in (True, False):
+                for k in (1, 2, 3):
+                    @pl.when((g + k < NG) == later)
+                    def _():
+                        high_copy(e, k, (g + k) % NG, g).start()
             high_in[e, g] = low_tot[e]
             third(low_in, e, low_pre)
 
-    def up_high(e):
+    def high_wait(e, s):
+        high_copy(e, 0, s, s).wait_recv()
+
+    def through_hubs(e):
         @pl.when(is_hub)
         def _():
-            for k in (1, 2, 3):
-                origin = (g + k) % NG
-                high_copy(e, k, origin, origin).wait_recv()
-            joint(high_in, e, high_pre, high_tot)
-            for k in (2, 1, 3):
-                @pl.when(y + k < NY)
-                def _():
-                    y_copy(e, k, (y + k) % NY, y).start()
-            third(high_in, e, high_pre)
-
-    def down_high(e):
-        @pl.when(is_hub)
-        def _():
+            for s in (0, 1, 2):
+                @pl.when(g > s)
+                def _():
+                    high_wait(e, s)
+                    high_tot[e] = high_in[e, 0] if s == 0 else compose(high_in[e, s], high_tot[e])
+
             start[e] = jnp.zeros((D, D), f32)
-            for s in (0, 1, 2):
+
+            @pl.when(y > 0)
+            def _():
+                y_copy_first(e, 0, 0).wait_recv()
+                start[e] = y_in[e, 0, :, D:]
+
+            for s in (1, 2):
                 @pl.when(y > s)
                 def _():
                     y_copy(e, 0, s, s).wait_recv()
@@ -311,7 +330,7 @@
 
             @pl.when(g > 0)
             def _():
-                start[e] = advance(high_pre[e, g - 1], start[e])
+                start[e] = advance(high_tot[e], start[e])
 
             begin = start[e]
             for place in range(NL):
@@ -324,6 +343,24 @@
                 @pl.when(l == place)
                 def _():
                     low_state[e] = low_out[e, place]
+
+            for s in range(NG):
+                @pl.when(s > g)
+                def _():
+                    high_wait(e, s)
+
+                @pl.when((s >= g) & (y < NY - 1))
+                def _():
+                    high_tot[e] = high_in[e, 0] if s == 0 else compose(high_in[e, s], high_tot[e])
+
+            for k in (1, 2, 3):
+                @pl.when(y == 0)
+                def _():
+                    y_copy_first(e, k, k).start()
+
+                @pl.when((y > 0) & (y + k < NY))
+                def _():
+                    y_copy(e, k, (y + k) % NY, y).start()
 
     def down_row(e):
         @pl.when(l != hub)
@@ -370,9 +407,11 @@
         ]
         keys = [k_ref[8 * half + i] for i in here]
         ys, maps = local_solves(keys, [v_ref[8 * half + i] for i in here], betas)
-        for i, (a_part, b_part) in zip(here, maps):
+        for i, (a_part, b_part), (hi, lo) in zip(here, maps, ys):
             pool[half, i, :, :D] = a_part
             pool[half, i, :, D:] = b_part
+            y_high[8 * half + i] = hi
+            y_low[8 * half + i] = lo
 
         @pl.when(t == 0)
         def _():
@@ -396,11 +435,6 @@
         def _():
             gain_copy().start()
 
-        outs = local_outputs([q_ref[8 * half + i] for i in here], keys, ys)
-        for i, (q_part, o_part) in zip(here, outs):
-            qo_ref[8 * half + i, :, :D] = q_part
-            qo_ref[8 * half + i, :, D:] = o_part
-
         @pl.when(t == 1 + c)
         def _():
             join_chip(0)
@@ -412,6 +446,15 @@
         return carry
 
     lax.fori_loop(0, 4, turn, 0)
+
+    def local_out(first):
+        here = [first + 2 * v for v in range(NX)]
+        outs = local_outputs(
+            [q_ref[h] for h in here], [k_ref[h] for h in here], [(y_high[h], y_low[h]) for h in here]
+        )
+        for h, (q_part, o_part) in zip(here, outs):
+            qo_ref[h, :, :D] = q_part
+            qo_ref[h, :, D:] = o_part
 
     def on_core(which, step):
         @pl.when(c == which)
@@ -423,17 +466,18 @@
     remote(gain_ref, gains_ref.at[2 * x + oc], GAIN, GAIN, partner).wait_recv()
     for k in (1, 2, 3):
         gain_row_copy(k, (x + k) % NX, x).start()
+    local_out(0)
     on_core(0, lambda: up_low(0))
     up_row(1)
     on_core(1, lambda: up_low(0))
-    on_core(0, lambda: up_high(0))
+    local_out(1)
     up_low(1)
-    on_core(1, lambda: up_high(0))
-    down_high(0)
-    up_high(1)
+    local_out(8)
+    through_hubs(0)
+    local_out(9)
     down_row(0)
     on_core(0, lambda: down_chip(0))
-    down_high(1)
+    through_hubs(1)
     on_core(1, lambda: down_chip(0))
     down_row(1)
     down_chip(1)
@@ -467,7 +511,11 @@
             for k in (1, 2, 3):
                 high_copy(e, k, (g + k) % NG, g).wait_send()
 
-                @pl.when(y + k < NY)
+                @pl.when(y == 0)
+                def _():
+                    y_copy_first(e, k, k).wait_send()
+
+                @pl.when((y > 0) & (y + k < NY))
                 def _():
                     y_copy(e, k, (y + k) % NY, y).wait_send()
 
@@ -492,9 +540,10 @@
             vm(3, 8, *wide), vm(8, *wide),
             vm(2, NX, *wide), vm(2, 3, *wide), vm(2, *wide),
             vm(2, NL, *wide), vm(2, 3, *wide), vm(2, *wide),
-            vm(2, NG, *wide), vm(2, 3, *wide), vm(2, *wide),
+            vm(2, NG, *wide), vm(2, *wide),
             vm(2, NY, *wide), vm(2, *square), vm(2, NL, *square), vm(2, *square),
             vm(2, NX, *square), vm(8, *square), vm(8, *square),
+            pltpu.VMEM((HEADS, N, 2 * D), bf16), pltpu.VMEM((HEADS, N, 2 * D), bf16),
             pltpu.SemaphoreType.DMA((SEMS,)), pltpu.SemaphoreType.DMA((SEMS,)), pltpu.SemaphoreType.REGULAR,
         ],
         compiler_params=pltpu.CompilerParams(

time: 83.8 us -> 88.8 us (1.060)
  Pallas kernels: 80.8 us -> 86.7 us
    pallas_call x1, Pallas kernels: 76.6 us -> 82.4 us  [states(): pl.pallas_call(states_kernel, in_specs=[whole] * 5, out_specs=[whole] * 3...]
where the time goes in v5:
time: 88.8 us; the launch traced here: 88.6 us
  Pallas kernels  86.7 us (98%)
  local copies, waits for them, and re-layouts  1.17 us (1%)
    pallas_call x1, Pallas kernels, states(): pl.pallas_call(states_kernel, in_specs=[whole] * 5, out_specs=[whole] * 3...  82.4 us
    pallas_call x1, Pallas kernels, by_head(): pl.pallas_call(by_head_kernel, in_specs=[away] * 3, out_specs=[whole] * 3...  2.18 us
    pallas_call x1, Pallas kernels, outputs(): pl.pallas_call(output_kernel, in_specs=[whole] * 4, out_specs=whole, out_...  2.05 us

profile of v5, /device:TPU:25, one launch (start us, length us, event | category | flops | bytes accessed | tf_op | source)
XLA Modules:
  0.0 88.6 jit_solution(13270331349338486320)
XLA Ops:
  0.0 0.0 copy-start.2
  0.0 0.7 convert_bitcast_fusion
  0.7 0.1 copy.7
  0.8 0.0 copy-start
  0.9 1.0 %copy-done = bf16[128,16,128]{2,1,0:T(8,128)(2,1)S(1)} copy-done((bf16[128,16,128]{2,1,0:T(8,128)(2,1)S(1)}, bf16[128,16,128]{2,1,0:T(8,128)(2,1)}, u32[]{:S(2)}) %copy-start) | copy-done | bytes 524312
  1.9 0.0 copy-start.1
  1.9 2.2 %shard_map.64 = (bf16[16,128,2,128]{3,2,1,0:T(2,128)(2,1)S(1)}, bf16[16,128,2,128]{3,2,1,0:T(2,128)(2,1)S(1)}, bf16[16,128,128]{2,1,0:T(8,128)(2,1)S(1)}) custom-call(bf16[128,16,2,128]{3,2,1,0:T(2,128)(2,1)} %k_ref.1, bf16[128,16,2,128]{3,2,1,0:T(2,128)(2,1)} %v_ref.1, bf16[128,16,128]{2,1,0:T(8,128)(2,1)S(1)} %copy-done), custom_call_target="tpu_custom_call" | custom-call | tf_op jit(solution)/shard_map/pallas_call | solution.py:574
  4.1 0.0 copy-done.2
  4.1 82.4 %shard_map.65 = (f32[16,128,256]{2,1,0:T(8,128)S(1)}, f32[16,128,128]{2,1,0:T(8,128)S(1)}, f32[8,2,128]{2,1,0:T(2,128)S(1)}) custom-call(bf16[16,256,128]{2,1,0:T(8,128)(2,1)S(1)} %bitcast.5, bf16[16,256,128]{2,1,0:T(8,128)(2,1)S(1)} %bitcast.6, bf16[16,128,128]{2,1,0:T(8,128)(2,1)S(1)} %get-tuple-element.13.q_ref, f32[256,16]{1,0:T(8,128)S(1)} %bitcast.7, ...), custom_call_target="tpu_custom_call" | custom-call | tf_op jit(solution)/shard_map/pallas_call | solution.py:530
  86.5 0.0 copy-done.1
  86.5 2.0 %shard_map.66 = bf16[128,16,128]{2,1,0:T(8,128)(2,1)} custom-call(f32[16,128,256]{2,1,0:T(8,128)S(1)} %get-tuple-element.14.qo_ref, f32[16,128,128]{2,1,0:T(8,128)S(1)} %get-tuple-element.15.m_ref, f32[8,2,128]{2,1,0:T(2,128)S(1)} %get-tuple-element.16.gains_ref, bf16[128,16,128]{2,1,0:T(8,128)(2,1)S(1)} %copy-done.1), custom_call_target="tpu_custom_call" | custom-call | tf_op jit(solution)/shard_map/pallas_call | solution.py:599
Async XLA Ops:
  0.0 4.1 %copy-start.2 = (f32[2,128]{1,0:T(2,128)S(1)}, f32[2,128]{1,0:T(2,128)}, u32[]{:S(2)}) copy-start(f32[2,128]{1,0:T(2,128)} %gain_ref.1) | copy-start | bytes 3076
  0.8 1.0 %copy-start = (bf16[128,16,128]{2,1,0:T(8,128)(2,1)S(1)}, bf16[128,16,128]{2,1,0:T(8,128)(2,1)}, u32[]{:S(2)}) copy-start(bf16[128,16,128]{2,1,0:T(8,128)(2,1)} %q_ref.1) | copy-start | bytes 1572868
  1.9 84.6 %copy-start.1 = (bf16[128,16,128]{2,1,0:T(8,128)(2,1)S(1)}, bf16[128,16,128]{2,1,0:T(8,128)(2,1)}, u32[]{:S(2)}) copy-start(bf16[128,16,128]{2,1,0:T(8,128)(2,1)} %gate_ref.1) | copy-start | bytes 1572868

commit v6 on v5

--- a/solution.py
+++ b/solution.py
@@ -293,8 +293,11 @@
                 origin = (l + k) % NL
                 low_copy(e, origin, origin).wait_recv()
             joint(low_in, e, low_pre, low_tot)
-            if e == 0:
+
+            @pl.when(e == 0)
+            def _():
                 pl.semaphore_wait(barrier, 6 - y)
+
             for later in (True, False):
                 for k in (1, 2, 3):
                     @pl.when((g + k < NG) == later)
@@ -399,7 +402,7 @@
 
     lane = lax.broadcasted_iota(jnp.int32, (N, HEADS), 1)
 
-    def turn(t, carry):
+    def turn(t):
         e, half = t // 2, t % 2
         here = [2 * v + e for v in range(NX)]
         betas = [
@@ -435,18 +438,6 @@
         def _():
             gain_copy().start()
 
-        @pl.when(t == 1 + c)
-        def _():
-            join_chip(0)
-
-        @pl.when((t == 2) & (c == 0))
-        def _():
-            up_row(0)
-
-        return carry
-
-    lax.fori_loop(0, 4, turn, 0)
-
     def local_out(first):
         here = [first + 2 * v for v in range(NX)]
         outs = local_outputs(
@@ -456,31 +447,45 @@
             qo_ref[h, :, :D] = q_part
             qo_ref[h, :, D:] = o_part
 
-    def on_core(which, step):
-        @pl.when(c == which)
-        def _():
-            step()
-
-    on_core(1, lambda: up_row(0))
-    join_chip(1)
-    remote(gain_ref, gains_ref.at[2 * x + oc], GAIN, GAIN, partner).wait_recv()
-    for k in (1, 2, 3):
-        gain_row_copy(k, (x + k) % NX, x).start()
-    local_out(0)
-    on_core(0, lambda: up_low(0))
-    up_row(1)
-    on_core(1, lambda: up_low(0))
-    local_out(1)
-    up_low(1)
-    local_out(8)
-    through_hubs(0)
-    local_out(9)
-    down_row(0)
-    on_core(0, lambda: down_chip(0))
-    through_hubs(1)
-    on_core(1, lambda: down_chip(0))
-    down_row(1)
-    down_chip(1)
+    def slot(it, carry):
+        @pl.when(it < 4)
+        def _():
+            turn(it)
+
+        @pl.when(it == 4)
+        def _():
+            remote(gain_ref, gains_ref.at[2 * x + oc], GAIN, GAIN, partner).wait_recv()
+            for k in (1, 2, 3):
+                gain_row_copy(k, (x + k) % NX, x).start()
+
+        @pl.when((it == 1 + c) | (it == 3 + c))
+        def _():
+            join_chip((it - 1 - c) // 2)
+
+        @pl.when((it == 2 + c) | (it == 4))
+        def _():
+            up_row(it // 4)
+
+        @pl.when((it == 3 + c) | (it == 5))
+        def _():
+            up_low(it // 5)
+
+        @pl.when((it == 5) | (it == 6))
+        def _():
+            through_hubs(it - 5)
+            down_row(it - 5)
+
+        @pl.when(it > 6)
+        def _():
+            down_chip(it - 7)
+
+        @pl.when((it > 3) & (it < 8))
+        def _():
+            local_out(8 * ((it - 4) // 2) + (it - 4) % 2)
+
+        return carry
+
+    lax.fori_loop(0, 9, slot, 0)
     for i in range(8):
         remote(after.at[i], m_ref.at[8 * oc + i], BACK + i, BACK + i, partner).wait_recv()
     for k in (1, 2, 3):

time: 88.8 us -> 88.7 us (level)
  no operation moved by 1% of the time
where the time goes in v6:
time: 88.7 us; the launch traced here: 88.4 us
  Pallas kernels  86.5 us (98%)
  local copies, waits for them, and re-layouts  1.17 us (1%)
    pallas_call x1, Pallas kernels, states(): pl.pallas_call(states_kernel, in_specs=[whole] * 5, out_specs=[whole] * 3...  82.3 us
    pallas_call x1, Pallas kernels, by_head(): pl.pallas_call(by_head_kernel, in_specs=[away] * 3, out_specs=[whole] * 3...  2.18 us
    pallas_call x1, Pallas kernels, outputs(): pl.pallas_call(output_kernel, in_specs=[whole] * 4, out_specs=whole, out_...  2.05 us

profile of v6, /device:TPU:25, one launch (start us, length us, event | category | flops | bytes accessed | tf_op | source)
XLA Modules:
  0.0 88.4 jit_solution(16573034184441817288)
XLA Ops:
  0.0 0.0 copy-start.2
  0.0 0.7 convert_bitcast_fusion
  0.7 0.1 copy.7
  0.8 0.0 copy-start
  0.9 1.0 %copy-done = bf16[128,16,128]{2,1,0:T(8,128)(2,1)S(1)} copy-done((bf16[128,16,128]{2,1,0:T(8,128)(2,1)S(1)}, bf16[128,16,128]{2,1,0:T(8,128)(2,1)}, u32[]{:S(2)}) %copy-start) | copy-done | bytes 524312
  1.9 0.0 copy-start.1
  1.9 2.2 %shard_map.64 = (bf16[16,128,2,128]{3,2,1,0:T(2,128)(2,1)S(1)}, bf16[16,128,2,128]{3,2,1,0:T(2,128)(2,1)S(1)}, bf16[16,128,128]{2,1,0:T(8,128)(2,1)S(1)}) custom-call(bf16[128,16,2,128]{3,2,1,0:T(2,128)(2,1)} %k_ref.1, bf16[128,16,2,128]{3,2,1,0:T(2,128)(2,1)} %v_ref.1, bf16[128,16,128]{2,1,0:T(8,128)(2,1)S(1)} %copy-done), custom_call_target="tpu_custom_call" | custom-call | tf_op jit(solution)/shard_map/pallas_call | solution.py:579
  4.1 0.0 copy-done.2
  4.1 82.3 %shard_map.65 = (f32[16,128,256]{2,1,0:T(8,128)S(1)}, f32[16,128,128]{2,1,0:T(8,128)S(1)}, f32[8,2,128]{2,1,0:T(2,128)S(1)}) custom-call(bf16[16,256,128]{2,1,0:T(8,128)(2,1)S(1)} %bitcast.5, bf16[16,256,128]{2,1,0:T(8,128)(2,1)S(1)} %bitcast.6, bf16[16,128,128]{2,1,0:T(8,128)(2,1)S(1)} %get-tuple-element.13.q_ref, f32[256,16]{1,0:T(8,128)S(1)} %bitcast.7, ...), custom_call_target="tpu_custom_call" | custom-call | tf_op jit(solution)/shard_map/pallas_call | solution.py:535
  86.4 0.0 copy-done.1
  86.4 2.0 %shard_map.66 = bf16[128,16,128]{2,1,0:T(8,128)(2,1)} custom-call(f32[16,128,256]{2,1,0:T(8,128)S(1)} %get-tuple-element.14.qo_ref, f32[16,128,128]{2,1,0:T(8,128)S(1)} %get-tuple-element.15.m_ref, f32[8,2,128]{2,1,0:T(2,128)S(1)} %get-tuple-element.16.gains_ref, bf16[128,16,128]{2,1,0:T(8,128)(2,1)S(1)} %copy-done.1), custom_call_target="tpu_custom_call" | custom-call | tf_op jit(solution)/shard_map/pallas_call | solution.py:604
Async XLA Ops:
  0.0 4.1 %copy-start.2 = (f32[2,128]{1,0:T(2,128)S(1)}, f32[2,128]{1,0:T(2,128)}, u32[]{:S(2)}) copy-start(f32[2,128]{1,0:T(2,128)} %gain_ref.1) | copy-start | bytes 3076
  0.8 1.0 %copy-start = (bf16[128,16,128]{2,1,0:T(8,128)(2,1)S(1)}, bf16[128,16,128]{2,1,0:T(8,128)(2,1)}, u32[]{:S(2)}) copy-start(bf16[128,16,128]{2,1,0:T(8,128)(2,1)} %q_ref.1) | copy-start | bytes 1572868
  1.9 84.5 %copy-start.1 = (bf16[128,16,128]{2,1,0:T(8,128)(2,1)S(1)}, bf16[128,16,128]{2,1,0:T(8,128)(2,1)}, u32[]{:S(2)}) copy-start(bf16[128,16,128]{2,1,0:T(8,128)(2,1)} %gate_ref.1) | copy-start | bytes 1572868

commit v7 on v6

--- a/solution.py
+++ b/solution.py
@@ -135,7 +135,7 @@
 def states_kernel(
     k_ref, v_ref, q_ref, b_ref, gain_ref, qo_ref, m_ref, gains_ref,
     pool, chip, row_in, row_pre, row_tot, low_in, low_pre, low_tot,
-    high_in, high_tot, y_in, start, low_out, low_state,
+    high_in, high_tot, y_in, row_end, start, low_out, low_state,
     row_out, chip_state, after, y_high, y_low, send, recv, near,
 ):
     seq, head = lax.axis_index("seq"), lax.axis_index("head")
@@ -174,10 +174,10 @@
         greet([device(ll=(l + k) % NL) for k in (1, 2, 3)])
         greet([device(xx=(x + k) % NX, cc=oc) for k in (0, 1, 2, 3)])
         greet([device(gg=(g + k) % NG, ll=meet((g + k) % NG)) for k in (1, 2, 3)])
-        for k in (1, 2, 3):
-            @pl.when(y >= k)
-            def _():
-                greet([device(yy=(y + NY - k) % NY)])
+
+        @pl.when(y > 0)
+        def _():
+            greet([device(yy=(y + NY - 1) % NY)])
 
     @pl.when(l != hub)
     def _():
@@ -225,14 +225,8 @@
             device(gg=there, ll=meet(there)),
         )
 
-    def y_copy(e, k, there, origin):
-        return remote(high_tot.at[e], y_in.at[e, origin], YS + 4 * e + k, YS + 4 * e + origin, device(yy=there))
-
-    def y_copy_first(e, k, there):
-        part = pl.ds(D, D)
-        return remote(
-            high_tot.at[e, :, part], y_in.at[e, 0, :, part], YS + 4 * e + k, YS + 4 * e, device(yy=there)
-        )
+    def y_copy(e, there):
+        return remote(row_end.at[e], y_in.at[e], YS + e, YS + e, device(yy=there))
 
     def low_back(e, there):
         return remote(
@@ -296,7 +290,7 @@
 
             @pl.when(e == 0)
             def _():
-                pl.semaphore_wait(barrier, 6 - y)
+                pl.semaphore_wait(barrier, 4 - y // (NY - 1))
 
             for later in (True, False):
                 for k in (1, 2, 3):
@@ -322,14 +316,8 @@
 
             @pl.when(y > 0)
             def _():
-                y_copy_first(e, 0, 0).wait_recv()
-                start[e] = y_in[e, 0, :, D:]
-
-            for s in (1, 2):
-                @pl.when(y > s)
-                def _():
-                    y_copy(e, 0, s, s).wait_recv()
-                    start[e] = advance(y_in[e, s], start[e])
+                y_copy(e, (y + NY - 1) % NY).wait_recv()
+                start[e] = y_in[e]
 
             @pl.when(g > 0)
             def _():
@@ -347,6 +335,7 @@
                 def _():
                     low_state[e] = low_out[e, place]
 
+            row_end[e] = begin
             for s in range(NG):
                 @pl.when(s > g)
                 def _():
@@ -354,16 +343,11 @@
 
                 @pl.when((s >= g) & (y < NY - 1))
                 def _():
-                    high_tot[e] = high_in[e, 0] if s == 0 else compose(high_in[e, s], high_tot[e])
-
-            for k in (1, 2, 3):
-                @pl.when(y == 0)
-                def _():
-                    y_copy_first(e, k, k).start()
-
-                @pl.when((y > 0) & (y + k < NY))
-                def _():
-                    y_copy(e, k, (y + k) % NY, y).start()
+                    row_end[e] = advance(high_in[e, s], row_end[e])
+
+            @pl.when(y < NY - 1)
+            def _():
+                y_copy(e, (y + 1) % NY).start()
 
     def down_row(e):
         @pl.when(l != hub)
@@ -516,13 +500,9 @@
             for k in (1, 2, 3):
                 high_copy(e, k, (g + k) % NG, g).wait_send()
 
-                @pl.when(y == 0)
-                def _():
-                    y_copy_first(e, k, k).wait_send()
-
-                @pl.when((y > 0) & (y + k < NY))
-                def _():
-                    y_copy(e, k, (y + k) % NY, y).wait_send()
+            @pl.when(y < NY - 1)
+            def _():
+                y_copy(e, (y + 1) % NY).wait_send()
 
 
 def states(keys, values, queries, betas, gain):
@@ -546,7 +526,7 @@
             vm(2, NX, *wide), vm(2, 3, *wide), vm(2, *wide),
             vm(2, NL, *wide), vm(2, 3, *wide), vm(2, *wide),
             vm(2, NG, *wide), vm(2, *wide),
-            vm(2, NY, *wide), vm(2, *square), vm(2, NL, *square), vm(2, *square),
+            vm(2, *square), vm(2, *square), vm(2, *square), vm(2, NL, *square), vm(2, *square),
             vm(2, NX, *square), vm(8, *square), vm(8, *square),
             pltpu.VMEM((HEADS, N, 2 * D), bf16), pltpu.VMEM((HEADS, N, 2 * D), bf16),
             pltpu.SemaphoreType.DMA((SEMS,)), pltpu.SemaphoreType.DMA((SEMS,)), pltpu.SemaphoreType.REGULAR,

time: 88.7 us -> 87.1 us (0.982)
  Pallas kernels: 86.5 us -> 84.9 us
    pallas_call x1, Pallas kernels: 82.3 us -> 80.7 us  [states(): pl.pallas_call(states_kernel, in_specs=[whole] * 5, out_specs=[whole] * 3...]
where the time goes in v7:
time: 87.1 us; the launch traced here: 86.9 us
  Pallas kernels  84.9 us (97%)
  local copies, waits for them, and re-layouts  1.17 us (1%)
    pallas_call x1, Pallas kernels, states(): pl.pallas_call(states_kernel, in_specs=[whole] * 5, out_specs=[whole] * 3...  80.7 us
    pallas_call x1, Pallas kernels, by_head(): pl.pallas_call(by_head_kernel, in_specs=[away] * 3, out_specs=[whole] * 3...  2.18 us
    pallas_call x1, Pallas kernels, outputs(): pl.pallas_call(output_kernel, in_specs=[whole] * 4, out_specs=whole, out_...  2.05 us

profile of v7, /device:TPU:25, one launch (start us, length us, event | category | flops | bytes accessed | tf_op | source)
XLA Modules:
  0.0 86.9 jit_solution(1865167413212601843)
XLA Ops:
  0.0 0.0 copy-start.2
  0.0 0.7 convert_bitcast_fusion
  0.7 0.1 copy.7
  0.8 0.0 copy-start
  0.9 1.0 %copy-done = bf16[128,16,128]{2,1,0:T(8,128)(2,1)S(1)} copy-done((bf16[128,16,128]{2,1,0:T(8,128)(2,1)S(1)}, bf16[128,16,128]{2,1,0:T(8,128)(2,1)}, u32[]{:S(2)}) %copy-start) | copy-done | bytes 524312
  1.9 0.0 copy-start.1
  1.9 2.2 %shard_map.64 = (bf16[16,128,2,128]{3,2,1,0:T(2,128)(2,1)S(1)}, bf16[16,128,2,128]{3,2,1,0:T(2,128)(2,1)S(1)}, bf16[16,128,128]{2,1,0:T(8,128)(2,1)S(1)}) custom-call(bf16[128,16,2,128]{3,2,1,0:T(2,128)(2,1)} %k_ref.1, bf16[128,16,2,128]{3,2,1,0:T(2,128)(2,1)} %v_ref.1, bf16[128,16,128]{2,1,0:T(8,128)(2,1)S(1)} %copy-done), custom_call_target="tpu_custom_call" | custom-call | tf_op jit(solution)/shard_map/pallas_call | solution.py:559
  4.1 0.0 copy-done.2
  4.1 80.7 %shard_map.65 = (f32[16,128,256]{2,1,0:T(8,128)S(1)}, f32[16,128,128]{2,1,0:T(8,128)S(1)}, f32[8,2,128]{2,1,0:T(2,128)S(1)}) custom-call(bf16[16,256,128]{2,1,0:T(8,128)(2,1)S(1)} %bitcast.5, bf16[16,256,128]{2,1,0:T(8,128)(2,1)S(1)} %bitcast.6, bf16[16,128,128]{2,1,0:T(8,128)(2,1)S(1)} %get-tuple-element.13.q_ref, f32[256,16]{1,0:T(8,128)S(1)} %bitcast.7, ...), custom_call_target="tpu_custom_call" | custom-call | tf_op jit(solution)/shard_map/pallas_call | solution.py:515
  84.8 0.0 copy-done.1
  84.8 2.0 %shard_map.66 = bf16[128,16,128]{2,1,0:T(8,128)(2,1)} custom-call(f32[16,128,256]{2,1,0:T(8,128)S(1)} %get-tuple-element.14.qo_ref, f32[16,128,128]{2,1,0:T(8,128)S(1)} %get-tuple-element.15.m_ref, f32[8,2,128]{2,1,0:T(2,128)S(1)} %get-tuple-element.16.gains_ref, bf16[128,16,128]{2,1,0:T(8,128)(2,1)S(1)} %copy-done.1), custom_call_target="tpu_custom_call" | custom-call | tf_op jit(solution)/shard_map/pallas_call | solution.py:584
Async XLA Ops:
  0.0 4.1 %copy-start.2 = (f32[2,128]{1,0:T(2,128)S(1)}, f32[2,128]{1,0:T(2,128)}, u32[]{:S(2)}) copy-start(f32[2,128]{1,0:T(2,128)} %gain_ref.1) | copy-start | bytes 3076
  0.8 1.0 %copy-start = (bf16[128,16,128]{2,1,0:T(8,128)(2,1)S(1)}, bf16[128,16,128]{2,1,0:T(8,128)(2,1)}, u32[]{:S(2)}) copy-start(bf16[128,16,128]{2,1,0:T(8,128)(2,1)} %q_ref.1) | copy-start | bytes 1572868
  1.9 82.9 %copy-start.1 = (bf16[128,16,128]{2,1,0:T(8,128)(2,1)S(1)}, bf16[128,16,128]{2,1,0:T(8,128)(2,1)}, u32[]{:S(2)}) copy-start(bf16[128,16,128]{2,1,0:T(8,128)(2,1)} %gate_ref.1) | copy-start | bytes 1572868

commit v8 on v6

--- a/solution.py
+++ b/solution.py
@@ -135,7 +135,7 @@
 def states_kernel(
     k_ref, v_ref, q_ref, b_ref, gain_ref, qo_ref, m_ref, gains_ref,
     pool, chip, row_in, row_pre, row_tot, low_in, low_pre, low_tot,
-    high_in, high_tot, y_in, start, low_out, low_state,
+    high_in, high_pre, high_tot, y_in, start, low_out, low_state,
     row_out, chip_state, after, y_high, y_low, send, recv, near,
 ):
     seq, head = lax.axis_index("seq"), lax.axis_index("head")
@@ -312,12 +312,19 @@
     def through_hubs(e):
         @pl.when(is_hub)
         def _():
-            for s in (0, 1, 2):
-                @pl.when(g > s)
-                def _():
-                    high_wait(e, s)
-                    high_tot[e] = high_in[e, 0] if s == 0 else compose(high_in[e, s], high_tot[e])
-
+            for k in (1, 2, 3):
+                high_wait(e, (g + k) % NG)
+            joint(high_in, e, high_pre, high_tot)
+            for k in (1, 2, 3):
+                @pl.when(y == 0)
+                def _():
+                    y_copy_first(e, k, k).start()
+
+                @pl.when((y > 0) & (y + k < NY))
+                def _():
+                    y_copy(e, k, (y + k) % NY, y).start()
+
+            third(high_in, e, high_pre)
             start[e] = jnp.zeros((D, D), f32)
 
             @pl.when(y > 0)
@@ -333,7 +340,7 @@
 
             @pl.when(g > 0)
             def _():
-                start[e] = advance(high_tot[e], start[e])
+                start[e] = advance(high_pre[e, g - 1], start[e])
 
             begin = start[e]
             for place in range(NL):
@@ -346,24 +353,6 @@
                 @pl.when(l == place)
                 def _():
                     low_state[e] = low_out[e, place]
-
-            for s in range(NG):
-                @pl.when(s > g)
-                def _():
-                    high_wait(e, s)
-
-                @pl.when((s >= g) & (y < NY - 1))
-                def _():
-                    high_tot[e] = high_in[e, 0] if s == 0 else compose(high_in[e, s], high_tot[e])
-
-            for k in (1, 2, 3):
-                @pl.when(y == 0)
-                def _():
-                    y_copy_first(e, k, k).start()
-
-                @pl.when((y > 0) & (y + k < NY))
-                def _():
-                    y_copy(e, k, (y + k) % NY, y).start()
 
     def down_row(e):
         @pl.when(l != hub)
@@ -545,7 +534,7 @@
             vm(3, 8, *wide), vm(8, *wide),
             vm(2, NX, *wide), vm(2, 3, *wide), vm(2, *wide),
             vm(2, NL, *wide), vm(2, 3, *wide), vm(2, *wide),
-            vm(2, NG, *wide), vm(2, *wide),
+            vm(2, NG, *wide), vm(2, 3, *wide), vm(2, *wide),
             vm(2, NY, *wide), vm(2, *square), vm(2, NL, *square), vm(2, *square),
             vm(2, NX, *square), vm(8, *square), vm(8, *square),
             pltpu.VMEM((HEADS, N, 2 * D), bf16), pltpu.VMEM((HEADS, N, 2 * D), bf16),

time: 88.7 us -> 81.6 us (0.920)
  Pallas kernels: 86.5 us -> 78.6 us
    pallas_call x1, Pallas kernels: 82.3 us -> 74.4 us  [states(): pl.pallas_call(states_kernel, in_specs=[whole] * 5, out_specs=[whole] * 3...]
where the time goes in v8:
time: 81.6 us; the launch traced here: 80.6 us
  Pallas kernels  78.6 us (96%)
  local copies, waits for them, and re-layouts  1.17 us (1%)
    pallas_call x1, Pallas kernels, states(): pl.pallas_call(states_kernel, in_specs=[whole] * 5, out_specs=[whole] * 3...  74.4 us
    pallas_call x1, Pallas kernels, by_head(): pl.pallas_call(by_head_kernel, in_specs=[away] * 3, out_specs=[whole] * 3...  2.18 us
    pallas_call x1, Pallas kernels, outputs(): pl.pallas_call(output_kernel, in_specs=[whole] * 4, out_specs=whole, out_...  2.05 us

profile of v8, /device:TPU:25, one launch (start us, length us, event | category | flops | bytes accessed | tf_op | source)
XLA Modules:
  0.0 80.6 jit_solution(989625357020159274)
XLA Ops:
  0.0 0.0 copy-start.2
  0.0 0.7 convert_bitcast_fusion
  0.7 0.1 copy.7
  0.8 0.0 copy-start
  0.9 1.0 %copy-done = bf16[128,16,128]{2,1,0:T(8,128)(2,1)S(1)} copy-done((bf16[128,16,128]{2,1,0:T(8,128)(2,1)S(1)}, bf16[128,16,128]{2,1,0:T(8,128)(2,1)}, u32[]{:S(2)}) %copy-start) | copy-done | bytes 524312
  1.9 0.0 copy-start.1
  1.9 2.2 %shard_map.64 = (bf16[16,128,2,128]{3,2,1,0:T(2,128)(2,1)S(1)}, bf16[16,128,2,128]{3,2,1,0:T(2,128)(2,1)S(1)}, bf16[16,128,128]{2,1,0:T(8,128)(2,1)S(1)}) custom-call(bf16[128,16,2,128]{3,2,1,0:T(2,128)(2,1)} %k_ref.1, bf16[128,16,2,128]{3,2,1,0:T(2,128)(2,1)} %v_ref.1, bf16[128,16,128]{2,1,0:T(8,128)(2,1)S(1)} %copy-done), custom_call_target="tpu_custom_call" | custom-call | tf_op jit(solution)/shard_map/pallas_call | solution.py:568
  4.1 0.0 copy-done.2
  4.1 74.4 %shard_map.65 = (f32[16,128,256]{2,1,0:T(8,128)S(1)}, f32[16,128,128]{2,1,0:T(8,128)S(1)}, f32[8,2,128]{2,1,0:T(2,128)S(1)}) custom-call(bf16[16,256,128]{2,1,0:T(8,128)(2,1)S(1)} %bitcast.5, bf16[16,256,128]{2,1,0:T(8,128)(2,1)S(1)} %bitcast.6, bf16[16,128,128]{2,1,0:T(8,128)(2,1)S(1)} %get-tuple-element.13.q_ref, f32[256,16]{1,0:T(8,128)S(1)} %bitcast.7, ...), custom_call_target="tpu_custom_call" | custom-call | tf_op jit(solution)/shard_map/pallas_call | solution.py:524
  78.5 0.0 copy-done.1
  78.5 2.0 %shard_map.66 = bf16[128,16,128]{2,1,0:T(8,128)(2,1)} custom-call(f32[16,128,256]{2,1,0:T(8,128)S(1)} %get-tuple-element.14.qo_ref, f32[16,128,128]{2,1,0:T(8,128)S(1)} %get-tuple-element.15.m_ref, f32[8,2,128]{2,1,0:T(2,128)S(1)} %get-tuple-element.16.gains_ref, bf16[128,16,128]{2,1,0:T(8,128)(2,1)S(1)} %copy-done.1), custom_call_target="tpu_custom_call" | custom-call | tf_op jit(solution)/shard_map/pallas_call | solution.py:593
Async XLA Ops:
  0.0 4.1 %copy-start.2 = (f32[2,128]{1,0:T(2,128)S(1)}, f32[2,128]{1,0:T(2,128)}, u32[]{:S(2)}) copy-start(f32[2,128]{1,0:T(2,128)} %gain_ref.1) | copy-start | bytes 3076
  0.8 1.0 %copy-start = (bf16[128,16,128]{2,1,0:T(8,128)(2,1)S(1)}, bf16[128,16,128]{2,1,0:T(8,128)(2,1)}, u32[]{:S(2)}) copy-start(bf16[128,16,128]{2,1,0:T(8,128)(2,1)} %q_ref.1) | copy-start | bytes 1572868
  1.9 76.6 %copy-start.1 = (bf16[128,16,128]{2,1,0:T(8,128)(2,1)S(1)}, bf16[128,16,128]{2,1,0:T(8,128)(2,1)}, u32[]{:S(2)}) copy-start(bf16[128,16,128]{2,1,0:T(8,128)(2,1)} %gate_ref.1) | copy-start | bytes 1572868

commit v9 on v8

--- a/solution.py
+++ b/solution.py
@@ -136,7 +136,7 @@
     k_ref, v_ref, q_ref, b_ref, gain_ref, qo_ref, m_ref, gains_ref,
     pool, chip, row_in, row_pre, row_tot, low_in, low_pre, low_tot,
     high_in, high_pre, high_tot, y_in, start, low_out, low_state,
-    row_out, chip_state, after, y_high, y_low, send, recv, near,
+    row_out, chip_state, after, y_high, y_low, send, recv,
 ):
     seq, head = lax.axis_index("seq"), lax.axis_index("head")
     x, c = head // 2, head % 2
@@ -163,41 +163,31 @@
         )
 
     barrier = pltpu.get_barrier_semaphore()
-    rows = [device(xx=(x + k) % NX) for k in (1, 2, 3)]
 
     def greet(peers):
         for peer in peers:
             pl.semaphore_signal(barrier, inc=1, device_id=peer, device_id_type=MESH)
 
+    greet([partner] + [device(xx=(x + k) % NX) for k in (1, 2, 3)])
+
     @pl.when(is_hub)
     def _():
         greet([device(ll=(l + k) % NL) for k in (1, 2, 3)])
-        greet([device(xx=(x + k) % NX, cc=oc) for k in (0, 1, 2, 3)])
         greet([device(gg=(g + k) % NG, ll=meet((g + k) % NG)) for k in (1, 2, 3)])
-        for k in (1, 2, 3):
-            @pl.when(y >= k)
-            def _():
-                greet([device(yy=(y + NY - k) % NY)])
+        greet([device(yy=(y + k) % NY) for k in (1, 2, 3)])
 
     @pl.when(l != hub)
     def _():
-        greet(rows)
-
-    @pl.when((l != hub) & (l != 3 - hub))
-    def _():
-        greet([partner])
-
-    def near_met():
-        @pl.when((l != hub) & (l != 3 - hub))
+        greet([device(ll=hub)])
+
+    def peers_met():
+        @pl.when(is_hub)
+        def _():
+            pl.semaphore_wait(barrier, 13)
+
+        @pl.when(l != hub)
         def _():
             pl.semaphore_wait(barrier, 5)
-            pl.semaphore_signal(near, inc=1, device_id=device(ll=hub), device_id_type=MESH)
-
-        @pl.when(l == 3 - hub)
-        def _():
-            pl.semaphore_wait(barrier, 8)
-            pl.semaphore_signal(near, inc=1, device_id=device(ll=hub), device_id_type=MESH)
-            pl.semaphore_signal(near, inc=1, device_id=partner, device_id_type=MESH)
 
     gains_ref[head] = gain_ref[...]
 
@@ -294,22 +284,15 @@
                 low_copy(e, origin, origin).wait_recv()
             joint(low_in, e, low_pre, low_tot)
 
-            @pl.when(e == 0)
-            def _():
-                pl.semaphore_wait(barrier, 6 - y)
-
-            for later in (True, False):
-                for k in (1, 2, 3):
-                    @pl.when((g + k < NG) == later)
-                    def _():
-                        high_copy(e, k, (g + k) % NG, g).start()
+            for k in (2, 1, 3):
+                high_copy(e, k, (g + k) % NG, g).start()
             high_in[e, g] = low_tot[e]
             third(low_in, e, low_pre)
 
     def high_wait(e, s):
         high_copy(e, 0, s, s).wait_recv()
 
-    def through_hubs(e):
+    def up_high(e):
         @pl.when(is_hub)
         def _():
             for k in (1, 2, 3):
@@ -325,6 +308,10 @@
                     y_copy(e, k, (y + k) % NY, y).start()
 
             third(high_in, e, high_pre)
+
+    def down_high(e):
+        @pl.when(is_hub)
+        def _():
             start[e] = jnp.zeros((D, D), f32)
 
             @pl.when(y > 0)
@@ -407,18 +394,9 @@
 
         @pl.when(t == 0)
         def _():
-            near_met()
-
-        @pl.when((t == 1) & is_hub)
-        def _():
-            pl.semaphore_wait(near, 4)
-
-        @pl.when((t == 1) & is_hub & (c == 1))
-        def _():
-            for v in range(NX):
-                pair_copy(2 * v).start()
-
-        @pl.when((half != c) & ((t > 0) | (l != hub)))
+            peers_met()
+
+        @pl.when(half != c)
         def _():
             for i in here:
                 pair_copy(i).start()
@@ -461,12 +439,16 @@
 
         @pl.when((it == 5) | (it == 6))
         def _():
-            through_hubs(it - 5)
-            down_row(it - 5)
-
-        @pl.when(it > 6)
-        def _():
-            down_chip(it - 7)
+            up_high(it - 5)
+
+        @pl.when((it == 6) | (it == 7))
+        def _():
+            down_high(it - 6)
+            down_row(it - 6)
+
+        @pl.when(it > 7)
+        def _():
+            down_chip(it - 8)
 
         @pl.when((it > 3) & (it < 8))
         def _():
@@ -474,7 +456,7 @@
 
         return carry
 
-    lax.fori_loop(0, 9, slot, 0)
+    lax.fori_loop(0, 10, slot, 0)
     for i in range(8):
         remote(after.at[i], m_ref.at[8 * oc + i], BACK + i, BACK + i, partner).wait_recv()
     for k in (1, 2, 3):
@@ -538,7 +520,7 @@
             vm(2, NY, *wide), vm(2, *square), vm(2, NL, *square), vm(2, *square),
             vm(2, NX, *square), vm(8, *square), vm(8, *square),
             pltpu.VMEM((HEADS, N, 2 * D), bf16), pltpu.VMEM((HEADS, N, 2 * D), bf16),
-            pltpu.SemaphoreType.DMA((SEMS,)), pltpu.SemaphoreType.DMA((SEMS,)), pltpu.SemaphoreType.REGULAR,
+            pltpu.SemaphoreType.DMA((SEMS,)), pltpu.SemaphoreType.DMA((SEMS,)),
         ],
         compiler_params=pltpu.CompilerParams(
             collective_id=0, has_side_effects=True, vmem_limit_bytes=48 * 2**20

time: 81.6 us -> 79.1 us (0.969)
  Pallas kernels: 78.6 us -> 76.9 us
    pallas_call x1, Pallas kernels: 74.4 us -> 72.7 us  [states(): pl.pallas_call(states_kernel, in_specs=[whole] * 5, out_specs=[whole] * 3...]
where the time goes in v9:
time: 79.1 us; the launch traced here: 78.9 us
  Pallas kernels  76.9 us (97%)
  local copies, waits for them, and re-layouts  1.17 us (1%)
    pallas_call x1, Pallas kernels, states(): pl.pallas_call(states_kernel, in_specs=[whole] * 5, out_specs=[whole] * 3...  72.7 us
    pallas_call x1, Pallas kernels, by_head(): pl.pallas_call(by_head_kernel, in_specs=[away] * 3, out_specs=[whole] * 3...  2.18 us
    pallas_call x1, Pallas kernels, outputs(): pl.pallas_call(output_kernel, in_specs=[whole] * 4, out_specs=whole, out_...  2.05 us

profile of v9, /device:TPU:25, one launch (start us, length us, event | category | flops | bytes accessed | tf_op | source)
XLA Modules:
  0.0 78.9 jit_solution(11453441933206681808)
XLA Ops:
  0.0 0.0 copy-start.2
  0.0 0.7 convert_bitcast_fusion
  0.7 0.1 copy.7
  0.8 0.0 copy-start
  0.9 1.0 %copy-done = bf16[128,16,128]{2,1,0:T(8,128)(2,1)S(1)} copy-done((bf16[128,16,128]{2,1,0:T(8,128)(2,1)S(1)}, bf16[128,16,128]{2,1,0:T(8,128)(2,1)}, u32[]{:S(2)}) %copy-start) | copy-done | bytes 524312
  1.9 0.0 copy-start.1
  1.9 2.2 %shard_map.64 = (bf16[16,128,2,128]{3,2,1,0:T(2,128)(2,1)S(1)}, bf16[16,128,2,128]{3,2,1,0:T(2,128)(2,1)S(1)}, bf16[16,128,128]{2,1,0:T(8,128)(2,1)S(1)}) custom-call(bf16[128,16,2,128]{3,2,1,0:T(2,128)(2,1)} %k_ref.1, bf16[128,16,2,128]{3,2,1,0:T(2,128)(2,1)} %v_ref.1, bf16[128,16,128]{2,1,0:T(8,128)(2,1)S(1)} %copy-done), custom_call_target="tpu_custom_call" | custom-call | tf_op jit(solution)/shard_map/pallas_call | solution.py:550
  4.1 0.0 copy-done.2
  4.1 72.7 %shard_map.65 = (f32[16,128,256]{2,1,0:T(8,128)S(1)}, f32[16,128,128]{2,1,0:T(8,128)S(1)}, f32[8,2,128]{2,1,0:T(2,128)S(1)}) custom-call(bf16[16,256,128]{2,1,0:T(8,128)(2,1)S(1)} %bitcast.5, bf16[16,256,128]{2,1,0:T(8,128)(2,1)S(1)} %bitcast.6, bf16[16,128,128]{2,1,0:T(8,128)(2,1)S(1)} %get-tuple-element.13.q_ref, f32[256,16]{1,0:T(8,128)S(1)} %bitcast.7, ...), custom_call_target="tpu_custom_call" | custom-call | tf_op jit(solution)/shard_map/pallas_call | solution.py:506
  76.8 0.0 copy-done.1
  76.8 2.0 %shard_map.66 = bf16[128,16,128]{2,1,0:T(8,128)(2,1)} custom-call(f32[16,128,256]{2,1,0:T(8,128)S(1)} %get-tuple-element.14.qo_ref, f32[16,128,128]{2,1,0:T(8,128)S(1)} %get-tuple-element.15.m_ref, f32[8,2,128]{2,1,0:T(2,128)S(1)} %get-tuple-element.16.gains_ref, bf16[128,16,128]{2,1,0:T(8,128)(2,1)S(1)} %copy-done.1), custom_call_target="tpu_custom_call" | custom-call | tf_op jit(solution)/shard_map/pallas_call | solution.py:575
Async XLA Ops:
  0.0 4.1 %copy-start.2 = (f32[2,128]{1,0:T(2,128)S(1)}, f32[2,128]{1,0:T(2,128)}, u32[]{:S(2)}) copy-start(f32[2,128]{1,0:T(2,128)} %gain_ref.1) | copy-start | bytes 3076
  0.8 1.0 %copy-start = (bf16[128,16,128]{2,1,0:T(8,128)(2,1)S(1)}, bf16[128,16,128]{2,1,0:T(8,128)(2,1)}, u32[]{:S(2)}) copy-start(bf16[128,16,128]{2,1,0:T(8,128)(2,1)} %q_ref.1) | copy-start | bytes 1572868
  1.9 74.9 %copy-start.1 = (bf16[128,16,128]{2,1,0:T(8,128)(2,1)S(1)}, bf16[128,16,128]{2,1,0:T(8,128)(2,1)}, u32[]{:S(2)}) copy-start(bf16[128,16,128]{2,1,0:T(8,128)(2,1)} %gate_ref.1) | copy-start | bytes 1572868

commit v10 on v9

--- a/solution.py
+++ b/solution.py
@@ -136,7 +136,7 @@
     k_ref, v_ref, q_ref, b_ref, gain_ref, qo_ref, m_ref, gains_ref,
     pool, chip, row_in, row_pre, row_tot, low_in, low_pre, low_tot,
     high_in, high_pre, high_tot, y_in, start, low_out, low_state,
-    row_out, chip_state, after, y_high, y_low, send, recv,
+    row_out, chip_state, after, y_high, y_low, q_heads, send, recv,
 ):
     seq, head = lax.axis_index("seq"), lax.axis_index("head")
     x, c = head // 2, head % 2
@@ -298,7 +298,7 @@
             for k in (1, 2, 3):
                 high_wait(e, (g + k) % NG)
             joint(high_in, e, high_pre, high_tot)
-            for k in (1, 2, 3):
+            for k in (2, 3, 1):
                 @pl.when(y == 0)
                 def _():
                     y_copy_first(e, k, k).start()
@@ -408,7 +408,7 @@
     def local_out(first):
         here = [first + 2 * v for v in range(NX)]
         outs = local_outputs(
-            [q_ref[h] for h in here], [k_ref[h] for h in here], [(y_high[h], y_low[h]) for h in here]
+            [q_heads[h] for h in here], [k_ref[h] for h in here], [(y_high[h], y_low[h]) for h in here]
         )
         for h, (q_part, o_part) in zip(here, outs):
             qo_ref[h, :, :D] = q_part
@@ -449,6 +449,10 @@
         @pl.when(it > 7)
         def _():
             down_chip(it - 8)
+
+        @pl.when(it == 4)
+        def _():
+            q_heads[...] = jnp.swapaxes(q_ref[...].astype(f32), 0, 1).astype(bf16)
 
         @pl.when((it > 3) & (it < 8))
         def _():
@@ -519,7 +523,7 @@
             vm(2, NG, *wide), vm(2, 3, *wide), vm(2, *wide),
             vm(2, NY, *wide), vm(2, *square), vm(2, NL, *square), vm(2, *square),
             vm(2, NX, *square), vm(8, *square), vm(8, *square),
-            pltpu.VMEM((HEADS, N, 2 * D), bf16), pltpu.VMEM((HEADS, N, 2 * D), bf16),
+            pltpu.VMEM((HEADS, N, 2 * D), bf16), pltpu.VMEM((HEADS, N, 2 * D), bf16), pltpu.VMEM((HEADS, T, D), bf16),
             pltpu.SemaphoreType.DMA((SEMS,)), pltpu.SemaphoreType.DMA((SEMS,)),
         ],
         compiler_params=pltpu.CompilerParams(
@@ -528,9 +532,7 @@
     )(keys, values, queries, betas, gain)
 
 
-def by_head_kernel(k_ref, v_ref, q_ref, ko_ref, vo_ref, qo_ref, held, sem, q_sem):
-    fetch = pltpu.make_async_copy(q_ref, held, q_sem)
-    fetch.start()
+def by_head_kernel(k_ref, v_ref, ko_ref, vo_ref, sem):
     copies = [
         pltpu.make_async_copy(src.at[:, h], dst.at[h], sem.at[n, h])
         for h in range(HEADS)
@@ -538,26 +540,22 @@
     ]
     for copy in copies:
         copy.start()
-    fetch.wait()
-    qo_ref[...] = jnp.swapaxes(held[...].astype(f32), 0, 1).astype(bf16)
     for copy in copies:
         copy.wait()
 
 
-def by_head(keys, values, queries):
+def by_head(keys, values):
     whole, away = pl.BlockSpec(memory_space=pltpu.VMEM), pl.BlockSpec(memory_space=pl.ANY)
     pairs = jax.ShapeDtypeStruct((HEADS, T, 2, D), bf16)
-    k, v, q = pl.pallas_call(
+    k, v = pl.pallas_call(
         by_head_kernel,
-        in_specs=[away] * 3,
-        out_specs=[whole] * 3,
-        out_shape=[pairs, pairs, jax.ShapeDtypeStruct((HEADS, T, D), bf16)],
-        scratch_shapes=[
-            pltpu.VMEM((T, HEADS, D), bf16), pltpu.SemaphoreType.DMA((2, HEADS)), pltpu.SemaphoreType.DMA,
-        ],
-        compiler_params=pltpu.CompilerParams(vmem_limit_bytes=50 * 2**20),
-    )(keys, values, queries)
-    return k.reshape(HEADS, N, D), v.reshape(HEADS, N, D), q
+        in_specs=[away] * 2,
+        out_specs=[whole] * 2,
+        out_shape=[pairs, pairs],
+        scratch_shapes=[pltpu.SemaphoreType.DMA((2, HEADS))],
+        compiler_params=pltpu.CompilerParams(vmem_limit_bytes=51 * 2**20),
+    )(keys, values)
+    return k.reshape(HEADS, N, D), v.reshape(HEADS, N, D)
 
 
 def output_kernel(qo_ref, m_ref, gains_ref, gate_ref, out_ref, rows):
@@ -583,9 +581,9 @@
 
 
 def local(queries, keys, values, betas, gate, gain):
-    keys_h, values_h, queries_h = by_head(keys, values, queries)
+    keys_h, values_h = by_head(keys, values)
     betas_h = jnp.transpose(betas, (0, 2, 1)).reshape(N, HEADS).astype(f32)
-    qo, m, gains = states(keys_h, values_h, queries_h, betas_h, gain)
+    qo, m, gains = states(keys_h, values_h, queries, betas_h, gain)
     return outputs(qo, m, gains, gate)
 
 

time: 79.1 us -> 77.9 us (0.985)
  local copies, waits for them, and re-layouts: 1.17 us -> 0.14 us
    unnamed x6, local copies, waits for them, and re-layouts: 1.04 us -> 0.01 us
where the time goes in v10:
time: 77.9 us; the launch traced here: 77.8 us
  Pallas kernels  76.8 us (99%)
    pallas_call x1, Pallas kernels, states(): pl.pallas_call(states_kernel, in_specs=[whole] * 5, out_specs=[whole] * 3...  72.7 us
    pallas_call x1, Pallas kernels, by_head(): pl.pallas_call(by_head_kernel, in_specs=[away] * 2, out_specs=[whole] * 2...  2.14 us
    pallas_call x1, Pallas kernels, outputs(): pl.pallas_call(output_kernel, in_specs=[whole] * 4, out_specs=whole, out_...  2.03 us

profile of v10, /device:TPU:25, one launch (start us, length us, event | category | flops | bytes accessed | tf_op | source)
XLA Modules:
  0.0 77.8 jit_solution(16852967857249655333)
XLA Ops:
  0.0 0.0 copy-start.2
  0.0 0.0 copy-start
  0.0 0.8 convert_bitcast_fusion
  0.8 0.1 copy.7
  0.9 0.0 copy-start.1
  0.9 2.1 %shard_map.64 = (bf16[16,128,2,128]{3,2,1,0:T(2,128)(2,1)S(1)}, bf16[16,128,2,128]{3,2,1,0:T(2,128)(2,1)S(1)}) custom-call(bf16[128,16,2,128]{3,2,1,0:T(2,128)(2,1)} %k_ref.1, bf16[128,16,2,128]{3,2,1,0:T(2,128)(2,1)} %v_ref.1), custom_call_target="tpu_custom_call" | custom-call | tf_op jit(solution)/shard_map/pallas_call | solution.py:550
  3.1 0.0 copy-done.2
  3.1 0.0 copy-done
  3.1 72.7 %shard_map.65 = (f32[16,128,256]{2,1,0:T(8,128)S(1)}, f32[16,128,128]{2,1,0:T(8,128)S(1)}, f32[8,2,128]{2,1,0:T(2,128)S(1)}) custom-call(bf16[16,256,128]{2,1,0:T(8,128)(2,1)S(1)} %bitcast.5, bf16[16,256,128]{2,1,0:T(8,128)(2,1)S(1)} %bitcast.6, bf16[128,16,128]{2,1,0:T(8,128)(2,1)S(1)} %copy-done, f32[256,16]{1,0:T(8,128)S(1)} %bitcast.7, ...), custom_call_target="tpu_custom_call" | custom-call | tf_op jit(solution)/shard_map/pallas_call | solution.py:510
  75.8 0.0 copy-done.1
  75.8 2.0 %shard_map.66 = bf16[128,16,128]{2,1,0:T(8,128)(2,1)} custom-call(f32[16,128,256]{2,1,0:T(8,128)S(1)} %get-tuple-element.12.qo_ref, f32[16,128,128]{2,1,0:T(8,128)S(1)} %get-tuple-element.13.m_ref, f32[8,2,128]{2,1,0:T(2,128)S(1)} %get-tuple-element.14.gains_ref, bf16[128,16,128]{2,1,0:T(8,128)(2,1)S(1)} %copy-done.1), custom_call_target="tpu_custom_call" | custom-call | tf_op jit(solution)/shard_map/pallas_call | solution.py:573
Async XLA Ops:
  0.0 3.1 %copy-start.2 = (f32[2,128]{1,0:T(2,128)S(1)}, f32[2,128]{1,0:T(2,128)}, u32[]{:S(2)}) copy-start(f32[2,128]{1,0:T(2,128)} %gain_ref.1) | copy-start | bytes 3076
  0.0 3.1 %copy-start = (bf16[128,16,128]{2,1,0:T(8,128)(2,1)S(1)}, bf16[128,16,128]{2,1,0:T(8,128)(2,1)}, u32[]{:S(2)}) copy-start(bf16[128,16,128]{2,1,0:T(8,128)(2,1)} %q_ref.1) | copy-start | bytes 1572868
  0.9 74.9 %copy-start.1 = (bf16[128,16,128]{2,1,0:T(8,128)(2,1)S(1)}, bf16[128,16,128]{2,1,0:T(8,128)(2,1)}, u32[]{:S(2)}) copy-start(bf16[128,16,128]{2,1,0:T(8,128)(2,1)} %gate_ref.1) | copy-start | bytes 1572868
